TPU v7x, 256 devices: a whole 4x4x8 slice. The times are simulated.
256 devices in a mesh: lat: 8 (over z), lon: 16 (over x, y_hi, core), batch: 2 (over y_lo).
Axes of the slice: x: 4, y: 4 (y_hi: 2, y_lo: 2; y = y_hi * 2 + y_lo), z: 8, core: 2. Of those that a mesh axis runs over, the one named last changes fastest.
Arguments:
- field: bfloat16 [2, 128, 768, 256], P('batch', 'lat', 'lon'), may hold values from -6 to 6
- kernel0: bfloat16 [3, 3, 256, 256], replicated, may hold values from -0.125 to 0.125
- kernel1: bfloat16 [3, 3, 256, 256], replicated, may hold values from -0.125 to 0.125
- mixing: bfloat16 [256, 256], replicated, may hold values from -0.375 to 0.375
- gain: float32 [512, 512], replicated, may hold values from -12 to 12
- cotangent: bfloat16 [2, 128, 768, 256], P('batch', 'lat', 'lon'), may hold values from -6 to 6
Outputs:
- predicted: bfloat16 [2, 128, 768, 256], P('batch', 'lat', 'lon')
- grad_kernel0: float32 [589824], P(('lat', 'lon', 'batch'))
- grad_kernel1: float32 [589824], P(('lat', 'lon', 'batch'))
- grad_mixing: float32 [65536], P(('lat', 'lon', 'batch'))
- grad_gain: float32 [262144], P(('lat', 'lon', 'batch'))
All inputs are finite; a program needn't handle non-finite values.
Results may differ from a plain program's by a relative error of at most 0.027.
Values may be sent and summed in bfloat16 or wider, within the bound.
A program may use at most 64 MiB of HBM per device.

v0:
```python
from functools import partial
import math

import jax
import jax.numpy as jnp
from jax import lax
from jax.sharding import PartitionSpec as P

KL_DEV = 2
KM_DEV = 2


HIGHEST = lax.Precision.HIGHEST


def with_halo(block, sides, width, periodic):
    for axis, dim in sides:
        count = lax.axis_size(axis)
        forward = [(i, i + 1) for i in range(count - 1)]
        if periodic:
            forward.append((count - 1, 0))
        backward = [(target, source) for source, target in forward]
        low = lax.ppermute(
            lax.slice_in_dim(block, block.shape[dim] - width, None, axis=dim), axis, forward
        )
        high = lax.ppermute(lax.slice_in_dim(block, 0, width, axis=dim), axis, backward)
        block = jnp.concatenate([low, block, high], axis=dim)
    return block


def activate(preact):
    return jax.nn.gelu(preact, approximate=True)


def activate_grad(preact, upstream):
    return jax.vjp(activate, preact)[1](upstream)[0]


def block_sum(values, factor):
    lat_cells, lon_cells, channels = values.shape
    shaped = values.reshape((lat_cells // factor, factor, lon_cells // factor, factor, channels))
    return jnp.sum(shaped, axis=(1, 3))


def spread(values, factor):
    return jnp.repeat(jnp.repeat(values, factor, axis=0), factor, axis=1)


def pad_tile(values):
    widened = with_halo(values, (("lon", 1),), 1, True)
    return with_halo(widened, (("lat", 0),), 1, False)


def conv_padded(padded, kernel):
    return lax.conv_general_dilated(
        padded[None],
        kernel,
        (1, 1),
        "VALID",
        dimension_numbers=("NHWC", "HWIO", "NHWC"),
        preferred_element_type=jnp.float32,
    )[0]


def kernel_terms(padded, upstream):
    lat_cells, lon_cells, channels = upstream.shape
    flat_up = upstream.reshape(lat_cells * lon_cells, channels)
    tap_terms = []
    for row_tap in range(3):
        for col_tap in range(3):
            window = padded[row_tap : row_tap + lat_cells, col_tap : col_tap + lon_cells].reshape(
                lat_cells * lon_cells, padded.shape[-1]
            )
            tap_terms.append(
                lax.dot_general(
                    window, flat_up, (((0,), (0,)), ((), ())), preferred_element_type=jnp.float32
                )
            )
    return jnp.stack(tap_terms)


def lat_tables(row_ids, lat_total, lat_modes):
    freqs = jnp.arange(lat_modes, dtype=jnp.int32) - lat_modes // 2
    phase = jnp.mod(freqs[:, None] * row_ids[None, :], lat_total).astype(jnp.float32) * (
        2.0 * math.pi / lat_total
    )
    return (jnp.cos(phase), jnp.sin(phase))


def lon_tables(col_ids, lon_total, lon_modes):
    freqs = jnp.arange(lon_modes, dtype=jnp.int32)
    phase = jnp.mod(col_ids[:, None] * freqs[None, :], lon_total).astype(jnp.float32) * (
        2.0 * math.pi / lon_total
    )
    return (jnp.cos(phase), jnp.sin(phase))


def analyse(source, lon_cos, lon_sin, lat_cos, lat_sin, weights):
    values = source.astype(jnp.float32)
    part_re = jnp.einsum("rjc,jm->rmc", values, lon_cos, precision=HIGHEST) * weights[None, :, None]
    part_im = (
        -jnp.einsum("rjc,jm->rmc", values, lon_sin, precision=HIGHEST) * weights[None, :, None]
    )
    coef_re = jnp.einsum("lr,rmc->lmc", lat_cos, part_re, precision=HIGHEST) + jnp.einsum(
        "lr,rmc->lmc", lat_sin, part_im, precision=HIGHEST
    )
    coef_im = jnp.einsum("lr,rmc->lmc", lat_cos, part_im, precision=HIGHEST) - jnp.einsum(
        "lr,rmc->lmc", lat_sin, part_re, precision=HIGHEST
    )
    return (coef_re, coef_im)


def synthesise(coef_re, coef_im, lat_cos, lat_sin, lon_cos, lon_sin, weights):
    sum_re = jnp.einsum("lr,lmc->rmc", lat_cos, coef_re, precision=HIGHEST) - jnp.einsum(
        "lr,lmc->rmc", lat_sin, coef_im, precision=HIGHEST
    )
    sum_im = jnp.einsum("lr,lmc->rmc", lat_cos, coef_im, precision=HIGHEST) + jnp.einsum(
        "lr,lmc->rmc", lat_sin, coef_re, precision=HIGHEST
    )
    scaled_re = sum_re * weights[None, :, None]
    scaled_im = sum_im * weights[None, :, None]
    return jnp.einsum("rmc,jm->rjc", scaled_re, lon_cos, precision=HIGHEST) - jnp.einsum(
        "rmc,jm->rjc", scaled_im, lon_sin, precision=HIGHEST
    )


def apply_gain(gain_re, gain_im, conj_sign, coef_re, coef_im, chan_start, chan_count):
    slice_re = lax.dynamic_slice_in_dim(gain_re, chan_start, chan_count, 2)
    slice_im = lax.dynamic_slice_in_dim(gain_im, chan_start, chan_count, 2) * conj_sign
    return (slice_re * coef_re - slice_im * coef_im, slice_re * coef_im + slice_im * coef_re)


def coarse_block(values, analysis_weights, synthesis_weights, mode_op):
    lat_local, lon_local, channels = values.shape
    lat_count = lax.axis_size("lat")
    lon_count = lax.axis_size("lon")
    lat_total = lat_local * lat_count
    lon_total = lon_local * lon_count
    lat_modes = KL_DEV * lat_count
    lon_modes = KM_DEV * lon_count
    own_rows = lax.axis_index("lat") * lat_local + jnp.arange(lat_local, dtype=jnp.int32)
    own_cols = lax.axis_index("lon") * lon_local + jnp.arange(lon_local, dtype=jnp.int32)
    all_cols = jnp.arange(lon_total, dtype=jnp.int32)
    own_cos, own_sin = lat_tables(own_rows, lat_total, lat_modes)
    chan_start = 0
    source = lax.all_gather(values, "lon", axis=1, tiled=True)
    cos_in, sin_in = lon_tables(all_cols, lon_total, lon_modes)
    coef_re, coef_im = analyse(source, cos_in, sin_in, own_cos, own_sin, analysis_weights)
    coef_re, coef_im = lax.psum((coef_re, coef_im), "lat")
    out_re, out_im = mode_op(coef_re, coef_im, chan_start, channels)
    cos_out, sin_out = lon_tables(own_cols, lon_total, lon_modes)
    result = synthesise(
        out_re, out_im, own_cos, own_sin, cos_out, sin_out, synthesis_weights
    ).astype(jnp.bfloat16)
    return (result, coef_re, coef_im, chan_start, channels)


def on_device(field, kernel0, kernel1, mixing, gain, cotangent):
    field_tile = field[0]
    upstream = cotangent[0].astype(jnp.float32)
    lat_cells, lon_cells, channels = field_tile.shape
    lat_count = lax.axis_size("lat")
    lon_count = lax.axis_size("lon")
    batch_count = lax.axis_size("batch")
    level_cells = batch_count * lat_cells * lat_count * lon_cells * lon_count
    padded0 = pad_tile(field_tile)
    preact0 = conv_padded(padded0, kernel0)
    level0 = (field_tile.astype(jnp.float32) + activate(preact0)).astype(jnp.bfloat16)
    coarse1 = (block_sum(level0.astype(jnp.float32), 2) / 4.0).astype(jnp.bfloat16)
    padded1 = pad_tile(coarse1)
    preact1 = conv_padded(padded1, kernel1)
    level1 = (coarse1.astype(jnp.float32) + activate(preact1)).astype(jnp.bfloat16)
    coarse2 = (block_sum(level1.astype(jnp.float32), 4) / 16.0).astype(jnp.bfloat16)
    lat_modes = KL_DEV * lat_count
    lon_modes = KM_DEV * lon_count
    norm_factor = 1.0 / math.sqrt(coarse2.shape[0] * lat_count * coarse2.shape[1] * lon_count)
    doubling = jnp.where(jnp.arange(lon_modes) == 0, 1.0, 2.0).astype(jnp.float32) * norm_factor
    uniform = jnp.full((lon_modes,), norm_factor, jnp.float32)
    gain_re = gain[:, :channels].reshape(lat_modes, lon_modes, channels)
    gain_im = gain[:, channels:].reshape(lat_modes, lon_modes, channels)
    filtered, spec_re, spec_im, chan_start, chan_count = coarse_block(
        coarse2, uniform, doubling, partial(apply_gain, gain_re, gain_im, 1.0)
    )
    flat_filtered = filtered.reshape(-1, channels)
    mixed_pre = jnp.dot(flat_filtered, mixing, preferred_element_type=jnp.float32).reshape(
        filtered.shape
    )
    level2 = (coarse2.astype(jnp.float32) + activate(mixed_pre)).astype(jnp.bfloat16)
    decoder = level1.astype(jnp.float32) + spread(level2.astype(jnp.float32), 4)
    predicted = (level0.astype(jnp.float32) + spread(decoder, 2)).astype(jnp.bfloat16)
    grad_dec = block_sum(upstream, 2)
    grad_level2 = block_sum(grad_dec, 4)
    grad_mixed = activate_grad(mixed_pre, grad_level2).astype(jnp.bfloat16)
    flat_grad = grad_mixed.reshape(-1, channels)
    mixing_term = lax.dot_general(
        flat_filtered, flat_grad, (((0,), (0,)), ((), ())), preferred_element_type=jnp.float32
    ) * (1.0 / math.sqrt(level_cells // 64))
    grad_filtered = (
        lax.dot_general(
            flat_grad, mixing, (((1,), (1,)), ((), ())), preferred_element_type=jnp.float32
        )
        .reshape(filtered.shape)
        .astype(jnp.bfloat16)
    )
    back_coarse, grad_re, grad_im, block_start, block_count = coarse_block(
        grad_filtered, doubling, uniform, partial(apply_gain, gain_re, gain_im, -1.0)
    )
    term_re = spec_re * grad_re + spec_im * grad_im
    term_im = spec_re * grad_im - spec_im * grad_re
    mode_rows = lat_modes * lon_modes
    empty_rows = jnp.zeros((mode_rows, channels), jnp.float32)
    full_re = lax.dynamic_update_slice_in_dim(
        empty_rows, term_re.reshape(mode_rows, chan_count), chan_start, 1
    )
    full_im = lax.dynamic_update_slice_in_dim(
        empty_rows, term_im.reshape(mode_rows, chan_count), chan_start, 1
    )
    gain_term = jnp.concatenate([full_re, full_im], axis=1)
    owner_id = lax.axis_index("lat") * lon_count + lax.axis_index("lon")
    owner_count = lat_count * lon_count
    row_owner = jnp.arange(mode_rows, dtype=jnp.int32) // (mode_rows // owner_count)
    gain_term = jnp.where((row_owner == owner_id)[:, None], gain_term, 0.0).reshape(-1)
    grad_level1 = grad_dec + spread(grad_level2 + back_coarse.astype(jnp.float32), 4) / 16.0
    grad_pre1 = activate_grad(preact1, grad_level1).astype(jnp.bfloat16)
    kernel1_term = kernel_terms(padded1, grad_pre1).reshape(-1) * (
        1.0 / math.sqrt(level_cells // 4)
    )
    flipped = jnp.transpose(kernel1[::-1, ::-1], (0, 1, 3, 2))
    grad_coarse1 = grad_level1 + conv_padded(pad_tile(grad_pre1), flipped)
    grad_level0 = upstream + spread(grad_coarse1, 2) / 4.0
    grad_pre0 = activate_grad(preact0, grad_level0).astype(jnp.bfloat16)
    kernel0_term = kernel_terms(padded0, grad_pre0).reshape(-1) * (1.0 / math.sqrt(level_cells))
    shallow_kernel, deep_kernel, deep_mixing, deep_gain = (
        lax.psum_scatter(kernel0_term, ("lat", "lon", "batch"), scatter_dimension=0, tiled=True),
        lax.psum_scatter(kernel1_term, ("lat", "lon", "batch"), scatter_dimension=0, tiled=True),
        lax.psum_scatter(
            mixing_term.reshape(-1), ("lat", "lon", "batch"), scatter_dimension=0, tiled=True
        ),
        lax.psum_scatter(gain_term, ("lat", "lon", "batch"), scatter_dimension=0, tiled=True),
    )
    return (predicted[None], shallow_kernel, deep_kernel, deep_mixing, deep_gain)


def solution(mesh):
    in_specs = (P("batch", "lat", "lon", None), P(), P(), P(), P(), P("batch", "lat", "lon", None))
    out_specs = (
        P("batch", "lat", "lon", None),
        P(("lat", "lon", "batch")),
        P(("lat", "lon", "batch")),
        P(("lat", "lon", "batch")),
        P(("lat", "lon", "batch")),
    )
    return jax.shard_map(
        on_device, mesh=mesh, in_specs=in_specs, out_specs=out_specs, check_vma=False
    )
```

profile of v0, /device:TPU:1, one launch (start us, length us, event | category | flops | bytes accessed | tf_op | source)
XLA Modules:
  0.0 593.4 jit_solution(11322150433231006432)
XLA Ops:
  7.2 1.0 fusion.323
  8.3 3.3 collective-permute-start.1
  11.6 1.2 collective-permute-start
  12.7 1.3 collective-permute-done.1
  14.1 1.3 collective-permute-done
  15.4 0.8 pad_maximum_fusion.12
  16.1 1.3 collective-permute-start.3
  17.4 4.2 collective-permute-start.2
  21.6 1.1 copy_convert_fusion.1
  23.5 0.9 pad
  24.4 1.2 reshape.177
  25.8 3.3 subtract_multiply_fusion
  29.4 0.9 slice.150
  30.4 2.5 reshape.266
  32.9 2.1 convert_reduce_fusion
  35.7 6.5 %collective-permute-start.5 = (bf16[8,1,256]{2,1,0:T(2,128)(2,1)S(1)}, bf16[8,1,256]{2,1,0:T(2,128)(2,1)S(1)}, u32[]{:S(2)}, u32[]{:S(2)}) collective-permute-start(bf16[8,1,256]{2,1,0:T(2,128)(2,1)S(1)} %get-tuple-element.69), channel_id=1, source_target_pairs={{2,0},{4,2},{6,4},{8,6},{10,8},{12,10},{14,12},{16,14},{18,16},{20... | collective-permute-start | bytes 12296 | tf_op jit(solution)/shard_map/ppermute | solution.py:26
  42.2 0.8 collective-permute-done.5
  43.4 1.3 collective-permute-start.7
  44.7 4.4 collective-permute-start.6
  50.7 1.7 convolution_select_fusion.2
  53.3 25.7 %all_gather.6 = bf16[2,96,256]{2,0,1:T(2,128)(2,1)S(1)} all-gather(bf16[2,6,256]{2,0,1:T(2,128)(2,1)S(1)} %copy.270), channel_id=1, replica_groups=mesh['lat'=8,'lon'=16,'batch'=2] {'lon'}, dimensions={1}, use_global_device_ids=true | all-gather | bytes 104448 | tf_op jit(solution)/shard_map/all_gather | solution.py:146
  81.1 1.6 convolution_subtract_fusion.1
  82.7 1.6 convolution_add_fusion.1
  84.3 1.0 copy_convert_fusion
  85.4 1.6 reshape.207
  88.8 1.3 fusion.322
  90.1 69.4 %all-reduce.15.cloned.1.call-done = (f32[16,32,256]{2,0,1:T(8,128)}, f32[16,32,256]{2,0,1:T(8,128)}) async-done(((f32[16,32,256]{2,0,1:T(8,128)}, f32[16,32,256]{2,0,1:T(8,128)}), (f32[16,32,256]{2,0,1:T(8,128)}, f32[16,32,256]{2,0,1:T(8,128)})) %all-reduce.15.cloned.1.call-update) | async-done | bytes 1048592 | tf_op jit(solution)/shard_map/psum | solution.py:149
  159.5 1.9 multiply_add_fusion.2
  161.4 1.1 fusion.263
  165.9 28.9 %all_gather.7 = bf16[2,96,256]{2,0,1:T(2,128)(2,1)S(1)} all-gather(bf16[2,6,256]{2,0,1:T(2,128)(2,1)S(1)} %copy.287), channel_id=1, replica_groups=mesh['lat'=8,'lon'=16,'batch'=2] {'lon'}, dimensions={1}, use_global_device_ids=true | all-gather | bytes 104448 | tf_op jit(solution)/shard_map/all_gather | solution.py:146
  196.8 1.6 convolution_subtract_fusion
  198.4 1.6 convolution_add_fusion
  200.9 2.5 copy.312
  203.4 1.2 copy.310
  204.6 1.2 copy.311
  205.9 1.4 pad_maximum_fusion
  207.3 0.8 pad_maximum_fusion.5
  208.8 1.7 reshape.167
  210.4 1.0 fusion.20
  211.4 0.8 copy.337
  212.3 53.0 %all-reduce.13.cloned.1.call-done = (f32[16,32,256]{2,0,1:T(8,128)}, f32[16,32,256]{2,0,1:T(8,128)}) async-done(((f32[16,32,256]{2,0,1:T(8,128)}, f32[16,32,256]{2,0,1:T(8,128)}), (f32[16,32,256]{2,0,1:T(8,128)}, f32[16,32,256]{2,0,1:T(8,128)})) %all-reduce.13.cloned.1.call-update) | async-done | bytes 1048592 | tf_op jit(solution)/shard_map/psum | solution.py:149
  265.2 3.3 multiply_add_fusion
  271.8 1.0 div.44
  272.8 1.8 fusion.108
  274.6 4.8 collective-permute-start.9
  279.5 2.7 collective-permute-start.8
  284.6 0.8 copy-done.13
  286.0 1.3 collective-permute-start.11
  287.3 4.2 collective-permute-start.10
  291.7 2.6 copy.336
  294.3 1.2 copy.338
  295.8 1.8 convolution_select_fusion.1
  298.1 1.0 broadcast_in_dim.82
  299.0 1.3 div.46
  300.9 1.3 fusion.9
  307.2 2.7 copy.335
  309.9 1.1 copy-done.18
  311.4 1.0 copy.283
  313.1 0.9 copy.321
  314.0 267.1 %all-reduce.11.cloned.1.call-done = (f32[589824]{0:T(1024)}, f32[589824]{0:T(1024)}, f32[65536]{0:T(1024)}, f32[262144]{0:T(1024)}) async-done(((f32[589824]{0:T(1024)}, f32[589824]{0:T(1024)}, f32[65536]{0:T(1024)}, f32[262144]{0:T(1024)}), (f32[589824]{0:T(1024)}, f32[589824]{0:T(1024)}, f32[65536]{0:T(1024)}, f32[262144]{0:T(1024)})) %all-reduce.11.cloned.1.call-update) | async-done | bytes 6029328
  581.0 1.4 dynamic-slice
  582.4 1.4 dynamic-slice.1
  583.8 1.3 dynamic-slice.2
  585.1 1.3 dynamic-slice.3
  (229 shorter events, 28.6 us)
Async XLA Ops:
  7.2 18.6 %copy-start = (bf16[3,3,256,256]{3,2,1,0:T(8,128)(2,1)S(1)}, bf16[3,3,256,256]{3,2,1,0:T(8,128)(2,1)}, u32[]{:S(2)}) copy-start(bf16[3,3,256,256]{3,2,1,0:T(8,128)(2,1)} %param.7) | copy-start | bytes 3538948
  7.2 16.1 %copy-start.1 = (bf16[1,16,48,256]{3,2,1,0:T(8,128)(2,1)S(1)}, bf16[1,16,48,256]{3,2,1,0:T(8,128)(2,1)}, u32[]{:S(2)}) copy-start(bf16[1,16,48,256]{3,2,1,0:T(8,128)(2,1)} %param.6) | copy-start | bytes 1179652
  7.2 152.3 %all-reduce.15.cloned.1.call-start = ((), (), s32[]{:S(2)}) async-start(), calls=%async_computation.2 | async-start | bytes 2097152 | tf_op jit(solution)/shard_map/psum | solution.py:149
  8.3 5.8 collective-permute-start.1
  11.6 3.8 collective-permute-start
  14.1 10.3 %copy-start.24 = (bf16[16,1,256]{2,1,0:T(2,128)(2,1)}, bf16[16,1,256]{2,1,0:T(2,128)(2,1)S(1)}, u32[]{:S(2)}) copy-start(bf16[16,1,256]{2,1,0:T(2,128)(2,1)S(1)} %collective-permute-done.1) | copy-start | bytes 24580
  15.4 9.0 %copy-start.27 = (bf16[16,1,256]{2,1,0:T(2,128)(2,1)}, bf16[16,1,256]{2,1,0:T(2,128)(2,1)S(1)}, u32[]{:S(2)}) copy-start(bf16[16,1,256]{2,1,0:T(2,128)(2,1)S(1)} %collective-permute-done) | copy-start | bytes 24580
  16.1 7.1 %collective-permute-start.3 = (bf16[1,50,256]{2,1,0:T(8,128)(2,1)S(1)}, bf16[1,50,256]{2,1,0:T(8,128)(2,1)S(1)}, u32[]{:S(2)}, u32[]{:S(2)}) collective-permute-start(bf16[1,50,256]{2,1,0:T(8,128)(2,1)S(1)} %get-tuple-element.55), channel_id=1, source_target_pairs={{32,0},{64,32},{96,64},{128,96},{160,128},{192,160},{224,192},{33,... | collective-permute-start | bytes 76808 | tf_op jit(solution)/shard_map/ppermute | solution.py:26
  17.4 5.8 collective-permute-start.2
  23.2 2.6 copy-start.58
  23.3 5.9 copy-start.36
  23.3 5.8 copy-start.38
  32.9 17.8 %copy-start.59 = (pred[8,4]{0,1:T(4,128)(4,1)S(1)}, pred[8,4]{0,1:T(4,128)(4,1)}, u32[]{:S(2)}) copy-start(pred[8,4]{0,1:T(4,128)(4,1)} %constant.147) | copy-start | bytes 100
  35.7 16.8 %copy-start.9 = (bf16[8,24,256]{2,1,0:T(8,128)(2,1)}, bf16[8,24,256]{2,1,0:T(8,128)(2,1)S(1)}, u32[]{:S(2)}) copy-start(bf16[8,24,256]{2,1,0:T(8,128)(2,1)S(1)} %multiply_convert_fusion) | copy-start | bytes 294916
  35.7 7.4 %collective-permute-start.5 = (bf16[8,1,256]{2,1,0:T(2,128)(2,1)S(1)}, bf16[8,1,256]{2,1,0:T(2,128)(2,1)S(1)}, u32[]{:S(2)}, u32[]{:S(2)}) collective-permute-start(bf16[8,1,256]{2,1,0:T(2,128)(2,1)S(1)} %get-tuple-element.69), channel_id=1, source_target_pairs={{2,0},{4,2},{6,4},{8,6},{10,8},{12,10},{14,12},{16,14},{18,16},{20... | collective-permute-start | bytes 12296 | tf_op jit(solution)/shard_map/ppermute | solution.py:26
  42.2 1.2 collective-permute-start.4
  43.1 7.1 %copy-start.40 = (bf16[8,1,256]{2,1,0:T(2,128)(2,1)}, bf16[8,1,256]{2,1,0:T(2,128)(2,1)S(1)}, u32[]{:S(2)}) copy-start(bf16[8,1,256]{2,1,0:T(2,128)(2,1)S(1)} %collective-permute-done.5) | copy-start | bytes 12292
  43.4 6.8 %copy-start.43 = (bf16[8,1,256]{2,1,0:T(2,128)(2,1)}, bf16[8,1,256]{2,1,0:T(2,128)(2,1)S(1)}, u32[]{:S(2)}) copy-start(bf16[8,1,256]{2,1,0:T(2,128)(2,1)S(1)} %collective-permute-done.4) | copy-start | bytes 12292
  43.4 5.8 collective-permute-start.7
  44.7 5.3 collective-permute-start.6
  49.2 33.5 %copy-start.33 = (s32[2]{0:T(128)}, s32[2]{0:T(128)S(1)}, u32[]{:S(2)}) copy-start(s32[2]{0:T(128)S(1)} %iota_add_fusion) | copy-start | bytes 28
  52.9 31.3 %copy-start.46 = (bf16[2,6,256]{2,1,0:T(8,128)(2,1)}, bf16[2,6,256]{2,1,0:T(8,128)(2,1)S(1)}, u32[]{:S(2)}) copy-start(bf16[2,6,256]{2,1,0:T(8,128)(2,1)S(1)} %multiply_convert_fusion.1) | copy-start | bytes 18436
  79.0 5.3 copy-start.2
  84.3 181.0 %all-reduce.13.cloned.1.call-start = ((), (), s32[]{:S(2)}) async-start(), calls=%async_computation.1 | async-start | bytes 2097152 | tf_op jit(solution)/shard_map/psum | solution.py:149
  159.5 3.0 copy-start.34
  159.5 3.5 copy-start.56
  159.5 4.5 copy-start.54
  159.5 5.0 copy-start.21
  159.5 5.0 copy-start.47
  200.1 381.0 %all-reduce.11.cloned.1.call-start = ((), (), s32[]{:S(2)}) async-start(), calls=%async_computation | async-start | bytes 12058624
  200.3 3.0 copy-start.20
  200.3 4.3 copy-start.19
  200.9 5.0 copy-start.25
  200.9 5.0 copy-start.28
  200.9 5.0 copy-start.37
  200.9 5.0 copy-start.39
  203.4 3.8 copy-start.10
  203.4 3.8 copy-start.41
  203.4 3.8 copy-start.44
  203.4 3.8 copy-start.50
  203.4 3.8 copy-start.52
  203.4 4.6 copy-start.53
  265.2 3.3 copy-start.35
  265.2 4.7 copy-start.55
  268.5 4.2 copy-start.8
  268.5 4.2 copy-start.15
  268.5 4.3 copy-start.17
  268.5 13.6 %copy-start.31 = (bf16[9,26,256]{2,1,0:T(8,128)(2,1)S(1)}, bf16[9,26,256]{2,1,0:T(8,128)(2,1)}, u32[]{:S(2)}) copy-start(bf16[9,26,256]{2,1,0:T(8,128)(2,1)} %get-tuple-element.61) | copy-start | bytes 359428
  271.0 11.9 %copy-start.11 = (bf16[8,24,256]{2,1,0:T(8,128)(2,1)S(1)}, bf16[8,24,256]{2,1,0:T(8,128)(2,1)}, u32[]{:S(2)}) copy-start(bf16[8,24,256]{2,1,0:T(8,128)(2,1)} %copy-done.9) | copy-start | bytes 294916
  271.0 11.9 %copy-start.45 = (bf16[8,1,256]{2,1,0:T(2,128)(2,1)S(1)}, bf16[8,1,256]{2,1,0:T(2,128)(2,1)}, u32[]{:S(2)}) copy-start(bf16[8,1,256]{2,1,0:T(2,128)(2,1)} %copy-done.43) | copy-start | bytes 12292
  274.6 8.8 %copy-start.42 = (bf16[8,1,256]{2,1,0:T(2,128)(2,1)S(1)}, bf16[8,1,256]{2,1,0:T(2,128)(2,1)}, u32[]{:S(2)}) copy-start(bf16[8,1,256]{2,1,0:T(2,128)(2,1)} %copy-done.40) | copy-start | bytes 12292
  274.6 11.4 %collective-permute-start.9 = (bf16[8,1,256]{2,1,0:T(2,128)(2,1)S(1)}, bf16[8,1,256]{2,1,0:T(2,128)(2,1)S(1)}, u32[]{:S(2)}, u32[]{:S(2)}) collective-permute-start(bf16[8,1,256]{2,1,0:T(2,128)(2,1)S(1)} %get-tuple-element.67), channel_id=1, source_target_pairs={{2,0},{4,2},{6,4},{8,6},{10,8},{12,10},{14,12},{16,14},{18,16},{20... | collective-permute-start | bytes 12296 | tf_op jit(solution)/shard_map/ppermute | solution.py:26
  279.5 6.6 %collective-permute-start.8 = (bf16[8,1,256]{2,1,0:T(2,128)(2,1)S(1)}, bf16[8,1,256]{2,1,0:T(2,128)(2,1)S(1)}, u32[]{:S(2)}, u32[]{:S(2)}) collective-permute-start(bf16[8,1,256]{2,1,0:T(2,128)(2,1)S(1)} %get-tuple-element.66), channel_id=1, source_target_pairs={{0,2},{2,4},{4,6},{6,8},{8,10},{10,12},{12,14},{14,16},{16,18},{18... | collective-permute-start | bytes 12296 | tf_op jit(solution)/shard_map/ppermute | solution.py:23
  282.4 1.2 copy-start.30
  284.3 1.3 copy-start.12
  284.3 7.3 %copy-start.57 = (pred[512]{0:T(512)(128)(4,1)S(1)}, pred[512]{0:T(512)(128)(4,1)}, u32[]{:S(2)}) copy-start(pred[512]{0:T(512)(128)(4,1)} %fusion.224) | copy-start | bytes 1540
  286.0 9.6 %collective-permute-start.11 = (bf16[1,26,256]{2,1,0:T(8,128)(2,1)S(1)}, bf16[1,26,256]{2,1,0:T(8,128)(2,1)S(1)}, u32[]{:S(2)}, u32[]{:S(2)}) collective-permute-start(bf16[1,26,256]{2,1,0:T(8,128)(2,1)S(1)} %get-tuple-element.63), channel_id=1, source_target_pairs={{32,0},{64,32},{96,64},{128,96},{160,128},{192,160},{224,192},{33,... | collective-permute-start | bytes 39944 | tf_op jit(solution)/shard_map/ppermute | solution.py:26
  287.3 8.3 %collective-permute-start.10 = (bf16[1,26,256]{2,1,0:T(8,128)(2,1)S(1)}, bf16[1,26,256]{2,1,0:T(8,128)(2,1)S(1)}, u32[]{:S(2)}, u32[]{:S(2)}) collective-permute-start(bf16[1,26,256]{2,1,0:T(8,128)(2,1)S(1)} %get-tuple-element.62), channel_id=1, source_target_pairs={{0,32},{32,64},{64,96},{96,128},{128,160},{160,192},{192,224},{1,3... | collective-permute-start | bytes 39944 | tf_op jit(solution)/shard_map/ppermute | solution.py:23
  294.3 1.4 copy-start.60
  295.8 4.5 copy-start.3
  300.3 2.0 copy-start.23
  302.3 1.4 copy-start.5
  302.3 1.7 copy-start.6
  303.1 1.4 copy-start.29
  (12 other events, 10.5 us)
Sparse Core Ops, SparseCore 0:
  84.4 75.0 all-reduce.14
  200.2 64.9 all-reduce.12
  310.0 270.9 all-reduce.10
where the time goes:
time: 602 us; the launch traced here: 593 us
  waiting for transfers between devices  394 us (65%)
  blocking collectives  54.6 us (9%)
  local copies, waits for them, and re-layouts  43.4 us (7%)
  starting transfers between devices  35.6 us (6%)
  matrix products  31.2 us (5%)
  other arithmetic  19.1 us (3%)
  between operations  15.5 us (3%)
    unnamed x4, waiting for transfers between devices  267 us
    psum x2, waiting for transfers between devices, coarse_block(): coef_re, coef_im = lax.psum((coef_re, coef_im), 'lat')  122 us
    all_gather x2, blocking collectives, coarse_block(): source = lax.all_gather(values, 'lon', axis=1, tiled=True)  54.6 us
    unnamed x131, local copies, waits for them, and re-layouts  18.6 us
    ppermute x6, starting transfers between devices, with_halo(): lax.ppermute(lax.slice_in_dim(block, 0, width, axis=dim), axis, backward)  18.6 us
    ppermute x6, starting transfers between devices, with_halo(): lax.ppermute(lax.slice_in_dim(block, block.shape[dim] - width, None, axis...  16.7 us
  transfers between devices with their start and end apart: 15, of which 8 were waited for; matrix products, arithmetic and copies ran while one was open for 5% of the time, Pallas kernels for 0%

commit v1 on v0

v1 whole, which is shorter than its diff:
```python
import functools
import math

import jax
import jax.numpy as jnp
import ml_dtypes
import numpy as np
from jax import lax
from jax.experimental import pallas as pl
from jax.experimental.pallas import tpu as pltpu
from jax.sharding import PartitionSpec as P

MESH = pl.DeviceIdType.MESH
F32 = jnp.float32
BF16 = jnp.bfloat16
C = 256
NLAT, NLON = 8, 16
ROWS, COLS = 16, 48
VMEM_BYTES = 56 * 2**20


def spectral_tables():
    lat_n, lon_n, kl, km = 16, 96, 16, 32
    freq = np.repeat(np.arange(kl) - kl // 2, km)
    mode = np.tile(np.arange(km), kl)
    norm = 1.0 / math.sqrt(lat_n * lon_n)

    def phase(i, j):
        whole = (freq[:, None] * i[None] * lon_n + mode[:, None] * j[None] * lat_n) % (lat_n * lon_n)
        return 2.0 * np.pi * whole / (lat_n * lon_n)

    forward = np.zeros((2, kl * km, NLON, NLAT, 2, 8))
    for lon in range(NLON):
        for lat in range(NLAT):
            for r in range(2):
                j = lon * 6 + np.arange(6)
                ph = phase(np.full(6, lat * 2 + r), j)
                forward[0, :, lon, lat, r, 1:7] = np.cos(ph) * norm
                forward[1, :, lon, lat, r, 1:7] = -np.sin(ph) * norm
    forward = forward.reshape(2 * kl * km, NLON * NLAT * 16)
    weight = np.where(mode == 0, 1.0, 2.0) * norm
    back = np.zeros((NLAT * NLON, 32, 2, kl * km))
    for lat in range(NLAT):
        for lon in range(NLON):
            i = np.repeat(lat * 2 - 1 + np.arange(4), 8)
            j = np.tile(lon * 6 - 1 + np.arange(8), 4)
            ph = phase(i, j).T
            back[lat * NLON + lon, :, 0] = np.cos(ph) * weight
            back[lat * NLON + lon, :, 1] = -np.sin(ph) * weight
    back = back.reshape(NLAT * NLON, 32, 2 * kl * km)
    return forward.astype(ml_dtypes.bfloat16), back.astype(ml_dtypes.bfloat16)


def cell_tables():
    pool2 = np.zeros((32, 2, 64))
    for j in range(32):
        pool2[j, :, 2 * j : 2 * j + 2] = 0.25
    pool4 = np.zeros((8, 4, 32))
    for j in range(1, 7):
        pool4[j, :, 4 * j : 4 * j + 4] = 1 / 16
    dec = np.zeros((4, 32, 8, 48))
    for r in range(4):
        for j in range(24):
            dec[r, 4 + j, :, 8 * (j // 4) : 8 * (j // 4) + 8] += 1 / 16
            dec[r, 4 + j, 2 * r : 2 * r + 2, 2 * j : 2 * j + 2] += 1
    sum8 = np.zeros((8, 8, 48))
    for j in range(6):
        sum8[1 + j, :, 8 * j : 8 * j + 8] = 1
    pick = np.zeros((64, 8, 32))
    for half, row, col in ((0, 0, 4), (32, 7, 27)):
        for i in range(24):
            pick[half + i, row, 4 + i] = 1
        for r in range(8):
            pick[half + 24 + r, r, col] = 1
    place = np.zeros((10, 32, 10, 16))
    for j in range(24):
        place[0, 4 + j, j // 16, j % 16] = 1
        place[9, 4 + j, 2 + j // 16, j % 16] = 1
    for r in range(8):
        place[1 + r, 3, 4, 8 + r] = 1
        place[1 + r, 28, 5, 8 + r] = 1
    place[0, 3, 6, 7] = 1
    place[0, 28, 7, 0] = 1
    place[9, 3, 8, 7] = 1
    place[9, 28, 9, 0] = 1
    up4 = np.zeros((10, 32, 4, 8))
    for r in range(10):
        for j in range(32):
            up4[r, j, (r + 3) // 4, j // 4] = 1 / 16
    up2 = np.zeros((2, 48, 32))
    up8 = np.zeros((2, 48, 8))
    for j in range(48):
        up2[:, j, 4 + j // 2] = 1
        up8[:, j, 1 + j // 8] = 1
    shapes = dict(
        pool2=(pool2, (32, 128)), pool4=(pool4, (8, 128)), dec=(dec, (128, 384)), sum8=(sum8, (8, 384)),
        pick=(pick, (64, 256)), place=(place, (320, 160)), up4=(up4, (320, 32)), up2=(up2, (96, 32)),
        up8=(up8, (96, 8)),
    )
    return {k: v.reshape(s).astype(ml_dtypes.bfloat16) for k, (v, s) in shapes.items()}


def dot(a, b):
    return jnp.dot(a, b, preferred_element_type=F32)


def dot_rows(a, b):
    return lax.dot_general(a, b, (((0,), (0,)), ((), ())), preferred_element_type=F32)


def dot_cols(a, b):
    return lax.dot_general(a, b, (((1,), (1,)), ((), ())), preferred_element_type=F32)


def gelu_both(v):
    k, q = 0.7978845608028654, 0.044715
    sq = v * v
    t = jnp.tanh(k * (v * (1.0 + q * sq)))
    half = 0.5 * (1.0 + t)
    return v * half, half + (0.5 * v) * (1.0 - t * t) * (k * (1.0 + (3.0 * q) * sq))


def place():
    return lax.axis_index("lat"), lax.axis_index("lon"), lax.axis_index("batch")


def step(pos, by, n):
    return lax.rem(pos + (by + n), n)


def signal(lat, lon, batch):
    pl.semaphore_signal(
        pltpu.get_barrier_semaphore(), inc=1, device_id={"lat": lat, "lon": lon, "batch": batch}, device_id_type=MESH
    )


def remote(src, dst, send, recv, lat, lon, batch):
    return pltpu.make_async_remote_copy(
        src_ref=src, dst_ref=dst, send_sem=send, recv_sem=recv,
        device_id={"lat": lat, "lon": lon, "batch": batch}, device_id_type=MESH,
    )


NEIGHBOURS = ((1, 0), (-1, 0), (0, 1), (0, -1), (1, 1), (1, -1), (-1, 1), (-1, -1))


def halo_copies(field, ext, send, recv):
    lat, lon, batch = place()
    rows = {1: (pl.ds(13, 3), pl.ds(0, 3)), -1: (pl.ds(0, 3), pl.ds(19, 3)), 0: (pl.ds(0, 16), pl.ds(3, 16))}
    cols = {1: (pl.ds(32, 16), pl.ds(0, 16)), -1: (pl.ds(0, 16), pl.ds(64, 16)), 0: (pl.ds(0, 48), pl.ds(16, 48))}
    copies = []
    for i, (dlat, dlon) in enumerate(NEIGHBOURS):
        (src_r, dst_r), (src_c, dst_c) = rows[dlat], cols[dlon]
        copies.append(remote(
            field.at[src_r, src_c], ext.at[dst_r, dst_c], send.at[i], recv.at[i],
            step(lat, dlat, NLAT), step(lon, dlon, NLON), batch,
        ))
    return copies


def forward_kernel(
    field, cot, k0, k1, pool2, pool4, dec, sum8, pick,
    x3c, da0, level0, x13, p1, level1, slot, a1, gl2, edges,
    ext, fs, x3, l0f, c1s, send, recv, own_sem,
):
    lat, lon, batch = place()
    for dlat, dlon in NEIGHBOURS:
        signal(step(lat, dlat, NLAT), step(lon, dlon, NLON), batch)
    own = pltpu.make_async_copy(field, ext.at[pl.ds(3, 16), pl.ds(16, 48)], own_sem)
    own.start()
    pl.semaphore_wait(pltpu.get_barrier_semaphore(), 8)
    copies = halo_copies(field, ext, send, recv)
    for copy in copies:
        copy.start()
    for half in range(2):
        part = cot[8 * half : 8 * half + 8].reshape(384, C)
        a1[4 * half : 4 * half + 4] = dot(dec[...], part).reshape(4, 32, C)
        gl2[8 * half : 8 * half + 8] = dot(sum8[...], part)
    own.wait()
    for copy in copies:
        copy.wait()

    edge_top = lat == 0
    edge_bot = lat == NLAT - 1
    fs[3:19] = ext[3:19].astype(F32)
    fs[0:3] = jnp.where(edge_top, 0.0, ext[0:3].astype(F32))
    fs[19:22] = jnp.where(edge_bot, 0.0, ext[19:22].astype(F32))
    for b in range(3):
        x3[:, :, b * C : (b + 1) * C] = fs[:, 7 + b : 71 + b, :].astype(BF16)
        x3c[:, :, b * C : (b + 1) * C] = fs[2:20, 15 + b : 63 + b, :].astype(BF16)

    def rows4(i, _):
        y = 4 * i
        acc = dot(x3[pl.ds(y, 4)].reshape(256, 3 * C), k0[0])
        acc += dot(x3[pl.ds(y + 1, 4)].reshape(256, 3 * C), k0[1])
        acc += dot(x3[pl.ds(y + 2, 4)].reshape(256, 3 * C), k0[2])
        act, slope = gelu_both(acc)
        out = fs[pl.ds(y + 1, 4), 8:72, :] + act.reshape(4, 64, C)
        l0f[pl.ds(y, 4)] = out.astype(BF16)
        level0[pl.ds(y, 4)] = out[:, 8:56].astype(BF16)
        da0[pl.ds(y, 4)] = slope.reshape(4, 64, C)[:, 8:56].astype(BF16)
        return 0

    lax.fori_loop(0, 5, rows4, 0)

    c1s[...] = jnp.zeros_like(c1s)
    for y in range(10):
        row = dot(pool2[...], l0f[2 * y : 2 * y + 2].reshape(128, C)).astype(BF16).astype(F32)
        if y == 0:
            row = jnp.where(edge_top, 0.0, row)
        if y == 9:
            row = jnp.where(edge_bot, 0.0, row)
        c1s[y, 8:40, :] = row
    for b in range(3):
        x13[:, :, b * C : (b + 1) * C] = c1s[:, 7 + b : 39 + b, :].astype(BF16)
    pre = dot(x13[0:8].reshape(256, 3 * C), k1[0])
    pre += dot(x13[1:9].reshape(256, 3 * C), k1[1])
    pre += dot(x13[2:10].reshape(256, 3 * C), k1[2])
    act, _ = gelu_both(pre)
    col = lax.broadcasted_iota(jnp.int32, (8, 32, C), 1)
    mine = (col >= 4) & (col < 28)
    pre = jnp.where(mine, pre.reshape(8, 32, C), 0.0)
    p1[...] = pre
    lev1 = jnp.where(mine, c1s[1:9, 8:40, :] + act.reshape(8, 32, C), 0.0).astype(BF16)
    level1[...] = lev1
    for half in range(2):
        slot[8 * half : 8 * half + 8] = dot(pool4[...], lev1[4 * half : 4 * half + 4].reshape(128, C)).astype(BF16)
    edges[:, 0] = dot(pick[...], a1[...].reshape(256, C).astype(BF16)).astype(BF16).reshape(4, 16, C)
    edges[:, 1] = dot(pick[...], pre.reshape(256, C).astype(BF16)).astype(BF16).reshape(4, 16, C)


def greet_band():
    lat, lon, batch = place()
    for k in range(1, NLAT):
        signal(step(lat, k, NLAT), lon, batch)
    for k in range(1, NLON):
        signal(lat, step(lon, k, NLON), batch)


def gather_cells(slot, cells, own_sem, send1, recv1, send2, recv2):
    lat, lon, batch = place()
    own = pltpu.make_async_copy(slot, cells.at[lon, lat], own_sem)
    own.start()
    first = [
        remote(slot, cells.at[lon, lat], send1.at[k - 1], recv1.at[k - 1], step(lat, k, NLAT), lon, batch)
        for k in range(1, NLAT)
    ]
    for copy in first:
        copy.start()
    own.wait()
    for copy in first:
        copy.wait()
    second = [
        remote(cells.at[lon], cells.at[lon], send2.at[k - 1], recv2.at[k - 1], lat, step(lon, k, NLON), batch)
        for k in range(1, NLON)
    ]
    for copy in second:
        copy.start()
    return second


EDGE_SENDS = (
    ((1, 0), 2, 2, 0), ((-1, 0), 0, 2, 2), ((0, 1), 3, 1, 4), ((0, -1), 1, 1, 5),
    ((1, 1), 3, 1, 6), ((1, -1), 2, 1, 7), ((-1, 1), 1, 1, 8), ((-1, -1), 0, 1, 9),
)


def spectral_kernel(
    slot, edges, table, synth, gain, mixing, gl2,
    ring, slot2, spec_own, level2, mix_grad,
    cells, coef, synth_own, own_sem, send1, recv1, send2, recv2, send3, recv3, synth_sem,
):
    lat, lon, batch = place()
    fetch = pltpu.make_async_copy(synth.at[lat * NLON + lon], synth_own, synth_sem)
    fetch.start()
    greet_band()
    for dlat, dlon in NEIGHBOURS[4:]:
        signal(step(lat, dlat, NLAT), step(lon, dlon, NLON), batch)
    pl.semaphore_wait(pltpu.get_barrier_semaphore(), NLAT + NLON - 2 + 4)
    second = gather_cells(slot, cells, own_sem, send1, recv1, send2, recv2)
    edge = []
    for i, ((dlat, dlon), seg, n, at) in enumerate(EDGE_SENDS):
        edge.append(remote(
            edges.at[pl.ds(seg, n)], ring.at[pl.ds(at, n)], send3.at[i], recv3.at[i],
            step(lat, dlat, NLAT), step(lon, dlon, NLON), batch,
        ))
    for copy in edge:
        copy.start()
    for copy in second:
        copy.wait()
    spec = dot(table[...], cells[...].reshape(NLON * NLAT * 16, C))
    sr, si = spec[:512], spec[512:]
    gr, gi = gain[:, :C], gain[:, C:]
    coef[0:512] = (gr * sr - gi * si).astype(BF16)
    coef[512:1024] = (gr * si + gi * sr).astype(BF16)
    fetch.wait()
    filt = dot(synth_own[8:24], coef[...]).astype(BF16)
    mixed = dot(filt, mixing[...])
    act, slope = gelu_both(mixed)
    level2[...] = (slot[...].astype(F32) + act).astype(BF16)
    col = lax.rem(lax.broadcasted_iota(jnp.int32, (16, C), 0), 8)
    gm = jnp.where((col >= 1) & (col < 7), gl2[...] * slope, 0.0).astype(BF16)
    mix_grad[...] = dot_rows(filt, gm).astype(BF16)
    slot2[...] = dot_cols(gm, mixing[...]).astype(BF16)
    rows = lax.broadcasted_iota(jnp.int32, (8, 512), 0)
    row_at = lax.broadcasted_iota(jnp.int32, (8, 512), 1)
    sel = jnp.where(row_at == rows + 8 * ((lat * NLON + lon) // 2), 1.0, 0.0)
    spec_own[:, :C] = jnp.dot(sel, sr, preferred_element_type=F32, precision=lax.Precision.HIGHEST)
    spec_own[:, C:] = jnp.dot(sel, si, preferred_element_type=F32, precision=lax.Precision.HIGHEST)
    for copy in edge:
        copy.wait()


def store_rows(parts, block, first, offset):
    n = block.shape[0]
    at = 0
    while at < n:
        chunk, inside = divmod(first + at, 144)
        size = min(n - at, 144 - inside)
        parts[chunk, offset + inside : offset + inside + size, :] = block[at : at + size].astype(BF16)
        at += size


def backward_kernel(
    slot2, ring, table, synth, gain, spec_own, mix_grad, a1, p1, x13, k1, x3c, cot, da0, level0, level1, level2,
    place_m, up4, up2, up8,
    predicted, parts, gain_grad,
    cells, coef, synth_own, sc, g1s, xg, gp0, own_sem, send1, recv1, send2, recv2, synth_sem,
):
    lat, lon, batch = place()
    fetch = pltpu.make_async_copy(synth.at[lat * NLON + lon], synth_own, synth_sem)
    fetch.start()
    greet_band()
    pl.semaphore_wait(pltpu.get_barrier_semaphore(), NLAT + NLON - 2)
    second = gather_cells(slot2, cells, own_sem, send1, recv1, send2, recv2)
    for r in range(8):
        low = dot(up2[...], level1[r]) + dot(up8[...], level2[8 * (r // 4) : 8 * (r // 4) + 8])
        high = level0[2 * r + 2 : 2 * r + 4].astype(F32) + low.reshape(2, 48, C)
        predicted[2 * r : 2 * r + 2] = high.astype(BF16)
    for s in range(16):
        parts[s, 288:304, :] = mix_grad[16 * s : 16 * s + 16]
    a1f = dot(place_m[...], ring[:, 0].reshape(160, C)).reshape(10, 32, C)
    p1f = dot(place_m[...], ring[:, 1].reshape(160, C)).reshape(10, 32, C)
    g1s[...] = jnp.zeros_like(g1s)
    g1s[:, 8:40, :] = a1f
    g1s[1:9, 8:40, :] += a1[...]
    xg[...] = p1f
    xg[1:9] += p1[...]
    _, slope1 = gelu_both(xg[...])
    xg[...] = slope1
    for copy in second:
        copy.wait()

    sc[...] = dot(table[...], cells[...].reshape(NLON * NLAT * 16, C))
    gr, gi = gain[:, :C], gain[:, C:]
    er, ei = sc[0:512], sc[512:1024]
    coef[0:512] = (gr * er + gi * ei).astype(BF16)
    coef[512:1024] = (gr * ei - gi * er).astype(BF16)
    fetch.wait()
    back = dot(synth_own[...], coef[...]).astype(BF16)
    gl1 = g1s[:, 8:40, :] + dot(up4[...], back).reshape(10, 32, C)
    col = lax.broadcasted_iota(jnp.int32, (10, 32, C), 1)
    row = lax.broadcasted_iota(jnp.int32, (10, 32, C), 0)
    first = jnp.where(lat == 0, 1, 0)
    last = jnp.where(lat == NLAT - 1, 9, 10)
    valid = (col >= 3) & (col < 29) & (row >= first) & (row < last)
    gp1 = jnp.where(valid, gl1 * xg[...], 0.0).astype(BF16)
    g1s[:, 8:40, :] = gp1.astype(F32)
    mine = (col[1:9] >= 4) & (col[1:9] < 28)
    gown = jnp.where(mine, gp1[1:9].astype(F32), 0.0).astype(BF16).reshape(256, C)
    gc1 = gl1[1:9].reshape(256, C)
    for b in range(3):
        shifted = g1s[:, 7 + b : 39 + b, :].astype(BF16)
        for a in range(3):
            gc1 += dot_cols(
                shifted[a : a + 8].reshape(256, C), k1[2 - a, (2 - b) * C : (3 - b) * C, :]
            )
    high = gc1.astype(BF16)
    low = (gc1 - high.astype(F32)).astype(BF16)
    for r in range(8):
        up = dot(up2[...], high[32 * r : 32 * r + 32]) + dot(up2[...], low[32 * r : 32 * r + 32])
        gl0 = cot[2 * r : 2 * r + 2].astype(F32) + 0.25 * up.reshape(2, 48, C)
        gp0[2 * r : 2 * r + 2] = (gl0 * da0[2 * r + 2 : 2 * r + 4].astype(F32)).astype(BF16)
    for a in range(3):
        store_rows(parts, dot_rows(x13[a : a + 8].reshape(256, 3 * C), gown), 768 * a, 144)
    for a in range(3):
        store_rows(parts, dot_rows(x3c[a : a + 16].reshape(768, 3 * C), gp0[...].reshape(768, C)), 768 * a, 0)

    base = 8 * ((lat * NLON + lon) // 2)
    rows = lax.broadcasted_iota(jnp.int32, (8, 512), 0)
    sel = jnp.where(lax.broadcasted_iota(jnp.int32, (8, 512), 1) == rows + base, 1.0, 0.0)
    br = jnp.dot(sel, sc[0:512], preferred_element_type=F32, precision=lax.Precision.HIGHEST)
    bi = jnp.dot(sel, sc[512:1024], preferred_element_type=F32, precision=lax.Precision.HIGHEST)
    m = lax.rem(base + lax.broadcasted_iota(jnp.int32, (8, C), 0), 32)
    weight = jnp.where(m == 0, 1.0, 2.0)
    ar, ai = spec_own[:, :C], spec_own[:, C:]
    gain_grad[:, :C] = weight * (ar * br + ai * bi)
    gain_grad[:, C:] = weight * (ar * bi - ai * br)


def reduce_kernel(
    scales, parts, gain_in, total, gain_out,
    got1, acc1, got2, acc2, got3, acc3, blocks, got4, gain_got,
    send1, recv1, send2, recv2, send3, recv3, send4, recv4, sendg, recvg,
):
    lat, lon, batch = place()
    core = lax.rem(lon, 2)
    yh = lax.rem(lon // 2, 2)
    x = lon // 4
    other = lon + 1 - 2 * core
    chunk = core * 8 + x * 2 + batch
    me = (lat * NLON + lon) * 2 + batch
    holder = lat * 2 + yh
    want = lat * 2 + lon // 8
    is_own = chunk == want
    signal(lat, other, batch)
    for k in range(1, 4):
        signal(lat, step(lon, 4 * k, NLON), batch)
    signal(lat, lon, 1 - batch)
    w_core, w_x, w_batch = want // 8, lax.rem(want // 2, 4), lax.rem(want, 2)
    for h in range(16):
        src_lon = w_x * 4 + (h % 2) * 2 + w_core

        @pl.when(jnp.logical_not(is_own & (holder == h)))
        def _():
            signal(h // 2, src_lon, w_batch)

    pl.semaphore_wait(pltpu.get_barrier_semaphore(), 21 - jnp.where(is_own, 1, 0))
    swap = remote(gain_in, gain_got, sendg, recvg, lat, lon, 1 - batch)
    swap.start()
    one = remote(parts.at[pl.ds(8 - 8 * core, 8)], got1, send1, recv1, lat, other, batch)
    one.start()
    one.wait()

    def add1(i, _):
        acc1[i] = (parts[8 * core + i].astype(F32) + got1[i].astype(F32)).astype(BF16)
        return 0

    lax.fori_loop(0, 8, add1, 0)
    two = []
    for k in range(1, 4):
        there = lax.rem(x + k, 4)
        two.append(remote(
            acc1.at[pl.ds(2 * there, 2)], got2.at[k - 1], send2.at[k - 1], recv2.at[k - 1],
            lat, step(lon, 4 * k, NLON), batch,
        ))
    for copy in two:
        copy.start()
    for copy in two:
        copy.wait()
    for i in range(2):
        acc2[i] = (
            acc1[2 * x + i].astype(F32) + got2[0, i].astype(F32) + got2[1, i].astype(F32) + got2[2, i].astype(F32)
        ).astype(BF16)
    three = remote(acc2.at[1 - batch], got3, send3, recv3, lat, lon, 1 - batch)
    three.start()
    three.wait()
    acc3[...] = acc2[batch].astype(F32) + got3[...].astype(F32)
    for e in range(16):
        block = jnp.concatenate(
            [acc3[9 * e : 9 * e + 9], acc3[144 + 9 * e : 153 + 9 * e], acc3[288 + e : 289 + e],
             jnp.zeros((13, C), F32)], axis=0
        )
        blocks[e] = block.astype(BF16)
    dest = 16 * chunk
    for e in range(16):
        to = dest + e
        copy = remote(
            blocks.at[e], got4.at[holder], send4.at[e], recv4.at[holder],
            to // 32, lax.rem(to // 2, NLON), e % 2,
        )

        @pl.when(to != me)
        def _():
            copy.start()

        @pl.when(to == me)
        def _():
            got4[holder] = blocks[e]

    for h in range(16):
        copy = remote(blocks.at[0], got4.at[h], send4.at[0], recv4.at[h], lat, other, batch)

        @pl.when(jnp.logical_not(is_own & (holder == h)))
        def _():
            copy.wait_recv()

    for e in range(16):
        copy = remote(blocks.at[e], got4.at[0], send4.at[e], recv4.at[0], lat, other, batch)

        @pl.when(dest + e != me)
        def _():
            copy.wait_send()

    acc = got4[0].astype(F32)
    for h in range(1, 16):
        acc += got4[h].astype(F32)
    s0, s1, s2 = scales
    row = lax.broadcasted_iota(jnp.int32, (32, C), 0)
    total[...] = acc * jnp.where(row < 9, s0, jnp.where(row < 18, s1, s2))
    swap.wait()
    gain_out[...] = gain_in[...] + gain_got[...]


def call(body, outs, scratch, collective, n_in, hbm=()):
    vmem = pl.BlockSpec(memory_space=pltpu.VMEM)
    anywhere = pl.BlockSpec(memory_space=pl.ANY)
    return pl.pallas_call(
        body,
        out_shape=[jax.ShapeDtypeStruct(s, d) for s, d in outs],
        in_specs=[anywhere if i in hbm else vmem for i in range(n_in)],
        out_specs=[vmem] * len(outs),
        scratch_shapes=scratch,
        compiler_params=pltpu.CompilerParams(
            collective_id=collective, has_side_effects=True, vmem_limit_bytes=VMEM_BYTES
        ),
    )


def dma(*n):
    return pltpu.SemaphoreType.DMA(n)


def on_device(tables, field, kernel0, kernel1, mixing, gain, cotangent):
    table, synth, small = tables
    small = {k: jnp.asarray(v) for k, v in small.items()}
    table, synth = jnp.asarray(table), jnp.asarray(synth)
    k0 = kernel0.reshape(3, 3 * C, C)
    k1 = kernel1.reshape(3, 3 * C, C)
    field, cot = field[0], cotangent[0]
    x3c, da0, level0, x13, p1, level1, slot, a1, gl2, edges = call(
        forward_kernel,
        [((18, 48, 3 * C), BF16), ((20, 48, C), BF16), ((20, 48, C), BF16), ((10, 32, 3 * C), BF16),
         ((8, 32, C), F32), ((8, 32, C), BF16), ((16, C), BF16), ((8, 32, C), F32), ((16, C), F32),
         ((4, 2, 16, C), BF16)],
        [pltpu.VMEM((22, 80, C), BF16), pltpu.VMEM((22, 80, C), F32), pltpu.VMEM((22, 64, 3 * C), BF16),
         pltpu.VMEM((20, 64, C), BF16), pltpu.VMEM((10, 48, C), F32), dma(8), dma(8), dma()],
        0, 9,
    )(field, cot, k0, k1, small["pool2"], small["pool4"], small["dec"], small["sum8"], small["pick"])
    ring, slot2, spec_own, level2, mix_grad = call(
        spectral_kernel,
        [((10, 2, 16, C), BF16), ((16, C), BF16), ((8, 2 * C), F32), ((16, C), BF16), ((C, C), BF16)],
        [pltpu.VMEM((NLON, NLAT, 16, C), BF16), pltpu.VMEM((1024, C), BF16), pltpu.VMEM((32, 1024), BF16),
         dma(), dma(7), dma(7), dma(15), dma(15), dma(8), dma(8), dma()],
        1, 7, hbm=(3,),
    )(slot, edges, table, synth, gain, mixing, gl2)
    predicted, parts, gain_grad = call(
        backward_kernel,
        [((ROWS, COLS, C), BF16), ((16, 304, C), BF16), ((8, 2 * C), F32)],
        [pltpu.VMEM((NLON, NLAT, 16, C), BF16), pltpu.VMEM((1024, C), BF16), pltpu.VMEM((32, 1024), BF16),
         pltpu.VMEM((1024, C), F32), pltpu.VMEM((10, 48, C), F32), pltpu.VMEM((10, 32, C), F32),
         pltpu.VMEM((16, 48, C), BF16), dma(), dma(7), dma(7), dma(15), dma(15), dma()],
        2, 21, hbm=(3,),
    )(slot2, ring, table, synth, gain, spec_own, mix_grad, a1, p1, x13, k1, x3c, cot, da0, level0, level1, level2,
      small["place"], small["up4"], small["up2"], small["up8"])
    cells0 = 2 * 128 * 768
    scales = (1.0 / math.sqrt(cells0), 1.0 / math.sqrt(cells0 // 4), 1.0 / math.sqrt(cells0 // 64))
    total, gain_sum = call(
        functools.partial(reduce_kernel, scales),
        [((32, C), F32), ((8, 2 * C), F32)],
        [pltpu.VMEM((8, 304, C), BF16), pltpu.VMEM((8, 304, C), BF16), pltpu.VMEM((3, 2, 304, C), BF16),
         pltpu.VMEM((2, 304, C), BF16), pltpu.VMEM((304, C), BF16), pltpu.VMEM((304, C), F32),
         pltpu.VMEM((16, 32, C), BF16), pltpu.VMEM((16, 32, C), BF16), pltpu.VMEM((8, 2 * C), F32),
         dma(), dma(), dma(3), dma(3), dma(), dma(), dma(16), dma(16), dma(), dma()],
        3, 2,
    )(parts, gain_grad)
    lat, lon, batch = place()
    at = 4 * lax.rem(lon, 2) + 2 * batch
    gain_rows = lax.dynamic_slice_in_dim(gain_sum, at, 2, 0)
    return (
        predicted[None], total[:9].reshape(-1), total[9:18].reshape(-1), total[18].reshape(-1),
        gain_rows.reshape(-1),
    )


def solution(mesh):
    tables = (*spectral_tables(), cell_tables())
    tile = P("batch", "lat", "lon", None)
    split = P(("lat", "lon", "batch"))
    return jax.shard_map(
        functools.partial(on_device, tables), mesh=mesh, in_specs=(tile, P(), P(), P(), P(), tile),
        out_specs=(tile, split, split, split, split), check_vma=False,
    )
```

time: 602 us -> 144 us (0.24)
  the two profiles are of different devices: /device:TPU:1 before, /device:TPU:31 now
where the time goes in v1:
time: 144 us
  Pallas kernels  138 us (96%)
  local copies, waits for them, and re-layouts  5.33 us (4%)
    pallas_call x1, Pallas kernels, on_device(): call(functools.partial(reduce_kernel, scales), [((32, C), F32), ((8, 2 *...  51.5 us
    pallas_call x1, Pallas kernels, on_device(): call(backward_kernel, [((ROWS, COLS, C), BF16), ((16, 304, C), BF16), ((8...  35.3 us
    pallas_call x1, Pallas kernels, on_device(): call(spectral_kernel, [((10, 2, 16, C), BF16), ((16, C), BF16), ((8, 2 *...  29.7 us
    pallas_call x1, Pallas kernels, on_device(): call(forward_kernel, [((18, 48, 3 * C), BF16), ((20, 48, C), BF16), ((20,...  21.6 us

profile of v1, /device:TPU:31, one launch (start us, length us, event | category | flops | bytes accessed | tf_op | source)
XLA Modules:
  0.0 144.1 jit_solution(2696878958134334962)
XLA Ops:
  0.6 21.6 %shard_map.200 = (bf16[18,48,768]{2,1,0:T(8,128)(2,1)}, bf16[20,48,256]{2,1,0:T(8,128)(2,1)}, bf16[20,48,256]{2,1,0:T(8,128)(2,1)}, bf16[10,32,768]{2,1,0:T(8,12...) custom-call(bf16[16,48,256]{2,1,0:T(8,128)(2,1)} %bitcast.14, ...), custom_call_target="tpu_custom_call" | custom-call | tf_op jit(solution)/shard_map/pallas_call | solution.py:531
  22.3 29.7 %shard_map.201 = (bf16[10,2,16,256]{3,2,1,0:T(8,128)(2,1)}, bf16[16,256]{1,0:T(8,128)(2,1)}, f32[8,512]{1,0:T(8,128)}, bf16[16,256]{1,0:T(8,128)(2,1)}, bf16[256,256]{1,0:T(8,128)(2,1)}) custom-call(bf16[16,256]{1,0:T(8,128)(2,1)} %get-tuple-element.25.slot, bf16[4,2,16,256]{3,2,1,0:T(8,128)(2,1)} %get-tuple-element.26.edges, ...), custom_call_target="tpu_custom_call" | custom-call | tf_op jit(solution)/shard_map/pallas_call | solution.py:540
  51.9 35.3 %shard_map.202 = (bf16[16,48,256]{2,1,0:T(8,128)(2,1)}, bf16[16,304,256]{2,1,0:T(8,128)(2,1)}, f32[8,512]{1,0:T(8,128)}) custom-call(bf16[16,256]{1,0:T(8,128)(2,1)} %get-tuple-element.28.slot2, bf16[10,2,16,256]{3,2,1,0:T(8,128)(2,1)} %get-tuple-element.29.ring, bf16[1024,2048]{1,0:T(8,128)(2,1)} %constant.50.clone.table, ...), custom_call_target="tpu_custom_call" | custom-call | tf_op jit(solution)/shard_map/pallas_call | solution.py:547
  87.3 0.0 copy-start
  87.3 51.5 %shard_map.203 = (f32[32,256]{1,0:T(8,128)}, f32[8,512]{1,0:T(8,128)}) custom-call(bf16[16,304,256]{2,1,0:T(8,128)(2,1)} %get-tuple-element.41.parts, f32[8,512]{1,0:T(8,128)} %get-tuple-element.42.gain_in), custom_call_target="tpu_custom_call" | custom-call | tf_op jit(solution)/shard_map/pallas_call | solution.py:558
  138.8 0.7 dynamic-slice_bitcast_fusion
  139.5 0.6 copy.22
  140.1 0.8 fusion
  140.9 0.6 reshape.27
  141.5 0.6 reshape.28
  142.1 1.3 slice.11
  143.3 0.0 copy-done
  143.3 0.7 copy.24
Async XLA Ops:
  87.3 56.1 %copy-start = (bf16[16,48,256]{2,1,0:T(8,128)(2,1)S(1)}, bf16[16,48,256]{2,1,0:T(8,128)(2,1)}, u32[]{:S(2)}) copy-start(bf16[16,48,256]{2,1,0:T(8,128)(2,1)} %get-tuple-element.40) | copy-start | bytes 1179652

commit v2 on v1

v2 whole, which is shorter than its diff:
```python
import functools
import math

import jax
import jax.numpy as jnp
import ml_dtypes
import numpy as np
from jax import lax
from jax.experimental import pallas as pl
from jax.experimental.pallas import tpu as pltpu
from jax.sharding import PartitionSpec as P

MESH = pl.DeviceIdType.MESH
F32 = jnp.float32
BF16 = jnp.bfloat16
C = 256
NLAT, NLON = 8, 16
ROWS, COLS = 16, 48
VMEM_BYTES = 56 * 2**20


def spectral_tables():
    lat_n, lon_n, kl, km = 16, 96, 16, 32
    freq = np.repeat(np.arange(kl) - kl // 2, km)
    mode = np.tile(np.arange(km), kl)
    norm = 1.0 / math.sqrt(lat_n * lon_n)

    def phase(i, j):
        whole = (freq[:, None] * i[None] * lon_n + mode[:, None] * j[None] * lat_n) % (lat_n * lon_n)
        return 2.0 * np.pi * whole / (lat_n * lon_n)

    forward = np.zeros((2, kl * km, NLON, NLAT, 2, 8))
    for lon in range(NLON):
        for lat in range(NLAT):
            for r in range(2):
                j = lon * 6 + np.arange(6)
                ph = phase(np.full(6, lat * 2 + r), j)
                forward[0, :, lon, lat, r, 1:7] = np.cos(ph) * norm
                forward[1, :, lon, lat, r, 1:7] = -np.sin(ph) * norm
    forward = forward.reshape(2 * kl * km, NLON * NLAT * 16)
    weight = np.where(mode == 0, 1.0, 2.0) * norm
    back = np.zeros((NLAT * NLON, 32, 2, kl * km))
    for lat in range(NLAT):
        for lon in range(NLON):
            i = np.repeat(lat * 2 - 1 + np.arange(4), 8)
            j = np.tile(lon * 6 - 1 + np.arange(8), 4)
            ph = phase(i, j).T
            back[lat * NLON + lon, :, 0] = np.cos(ph) * weight
            back[lat * NLON + lon, :, 1] = -np.sin(ph) * weight
    back = back.reshape(NLAT * NLON, 32, 2 * kl * km)
    forward = forward.reshape(2 * kl * km, 8, 256).transpose(1, 0, 2)
    return forward.astype(ml_dtypes.bfloat16), back.astype(ml_dtypes.bfloat16)


def cell_tables():
    pool2 = np.zeros((32, 2, 64))
    for j in range(32):
        pool2[j, :, 2 * j : 2 * j + 2] = 0.25
    pool4 = np.zeros((8, 4, 32))
    for j in range(1, 7):
        pool4[j, :, 4 * j : 4 * j + 4] = 1 / 16
    dec = np.zeros((4, 32, 8, 48))
    for r in range(4):
        for j in range(24):
            dec[r, 4 + j, :, 8 * (j // 4) : 8 * (j // 4) + 8] += 1 / 16
            dec[r, 4 + j, 2 * r : 2 * r + 2, 2 * j : 2 * j + 2] += 1
    sum8 = np.zeros((8, 8, 48))
    for j in range(6):
        sum8[1 + j, :, 8 * j : 8 * j + 8] = 1
    pick = np.zeros((64, 8, 32))
    for half, row, col in ((0, 0, 4), (32, 7, 27)):
        for i in range(24):
            pick[half + i, row, 4 + i] = 1
        for r in range(8):
            pick[half + 24 + r, r, col] = 1
    place = np.zeros((10, 32, 10, 16))
    for j in range(24):
        place[0, 4 + j, j // 16, j % 16] = 1
        place[9, 4 + j, 2 + j // 16, j % 16] = 1
    for r in range(8):
        place[1 + r, 3, 4, 8 + r] = 1
        place[1 + r, 28, 5, 8 + r] = 1
    place[0, 3, 6, 7] = 1
    place[0, 28, 7, 0] = 1
    place[9, 3, 8, 7] = 1
    place[9, 28, 9, 0] = 1
    up4 = np.zeros((10, 32, 4, 8))
    for r in range(10):
        for j in range(32):
            up4[r, j, (r + 3) // 4, j // 4] = 1 / 16
    up2 = np.zeros((2, 48, 32))
    up8 = np.zeros((2, 48, 8))
    for j in range(48):
        up2[:, j, 4 + j // 2] = 1
        up8[:, j, 1 + j // 8] = 1
    shapes = dict(
        pool2=(pool2, (32, 128)), pool4=(pool4, (8, 128)), dec=(dec, (128, 384)), sum8=(sum8, (8, 384)),
        pick=(pick, (64, 256)), place=(place, (320, 160)), up4=(up4, (320, 32)), up2=(up2, (96, 32)),
        up8=(up8, (96, 8)),
    )
    return {k: v.reshape(s).astype(ml_dtypes.bfloat16) for k, (v, s) in shapes.items()}


def dot(a, b):
    return jnp.dot(a, b, preferred_element_type=F32)


def dot_rows(a, b):
    return lax.dot_general(a, b, (((0,), (0,)), ((), ())), preferred_element_type=F32)


def dot_cols(a, b):
    return lax.dot_general(a, b, (((1,), (1,)), ((), ())), preferred_element_type=F32)


def gelu_both(v):
    k, q = 0.7978845608028654, 0.044715
    sq = v * v
    t = jnp.tanh(k * (v * (1.0 + q * sq)))
    half = 0.5 * (1.0 + t)
    return v * half, half + (0.5 * v) * (1.0 - t * t) * (k * (1.0 + (3.0 * q) * sq))


def place():
    return lax.axis_index("lat"), lax.axis_index("lon"), lax.axis_index("batch")


def step(pos, by, n):
    return lax.rem(pos + (by + n), n)


def signal(lat, lon, batch):
    pl.semaphore_signal(
        pltpu.get_barrier_semaphore(), inc=1, device_id={"lat": lat, "lon": lon, "batch": batch}, device_id_type=MESH
    )


def remote(src, dst, send, recv, lat, lon, batch):
    return pltpu.make_async_remote_copy(
        src_ref=src, dst_ref=dst, send_sem=send, recv_sem=recv,
        device_id={"lat": lat, "lon": lon, "batch": batch}, device_id_type=MESH,
    )


NEIGHBOURS = ((1, 0), (-1, 0), (0, 1), (0, -1), (1, 1), (1, -1), (-1, 1), (-1, -1))


def halo_copies(field, ext, send, recv):
    lat, lon, batch = place()
    rows = {1: (pl.ds(13, 3), pl.ds(0, 3)), -1: (pl.ds(0, 3), pl.ds(19, 3)), 0: (pl.ds(0, 16), pl.ds(3, 16))}
    cols = {1: (pl.ds(32, 16), pl.ds(0, 16)), -1: (pl.ds(0, 16), pl.ds(64, 16)), 0: (pl.ds(0, 48), pl.ds(16, 48))}
    copies = []
    for i, (dlat, dlon) in enumerate(NEIGHBOURS):
        (src_r, dst_r), (src_c, dst_c) = rows[dlat], cols[dlon]
        copies.append(remote(
            field.at[src_r, src_c], ext.at[dst_r, dst_c], send.at[i], recv.at[i],
            step(lat, dlat, NLAT), step(lon, dlon, NLON), batch,
        ))
    return copies


EDGE_SENDS = (
    ((1, 0), 2, 2, 0), ((-1, 0), 0, 2, 2), ((0, 1), 3, 1, 4), ((0, -1), 1, 1, 5),
    ((1, 1), 3, 1, 6), ((1, -1), 2, 1, 7), ((-1, 1), 1, 1, 8), ((-1, -1), 0, 1, 9),
)


def edge_copies(edges, ring, send, recv):
    lat, lon, batch = place()
    return [
        remote(
            edges.at[pl.ds(seg, n)], ring.at[pl.ds(at, n)], send.at[i], recv.at[i],
            step(lat, dlat, NLAT), step(lon, dlon, NLON), batch,
        )
        for i, ((dlat, dlon), seg, n, at) in enumerate(EDGE_SENDS)
    ]


def greet_all():
    lat, lon, batch = place()
    for k in range(1, NLAT):
        signal(step(lat, k, NLAT), lon, batch)
    for k in (1, -1):
        signal(lat, step(lon, k, NLON), batch)
    for dlat, dlon in NEIGHBOURS[4:]:
        signal(step(lat, dlat, NLAT), step(lon, dlon, NLON), batch)
    for k in range(1, 8):
        signal(lat, step(lon, 2 * k, NLON), batch)
    signal(lat, lon, 1 - batch)
    signal(lat, lon + 2 - 4 * lax.rem(lon // 2, 2), 1 - batch)
    return 22


class Gather:
    def __init__(self, slot, cells, own, send1, recv1, send2, recv2, send3, recv3):
        lat, lon, batch = place()
        self.q, self.core, self.cells = lon // 2, lax.rem(lon, 2), cells
        other = lon + 1 - 2 * self.core
        here = cells.at[self.q, self.core]
        self.own = pltpu.make_async_copy(slot, here.at[lat], own)
        self.first = [
            remote(slot, here.at[lat], send1.at[k - 1], recv1.at[k - 1], step(lat, k, NLAT), lon, batch)
            for k in range(1, NLAT)
        ]
        self.second = {
            k: remote(here, here, send2.at[k - 1], recv2.at[k - 1], lat, step(lon, 2 * k, NLON), batch)
            for k in range(1, 8)
        }
        self.third = {}
        for k in range(8):
            block = cells.at[lax.rem(self.q + 8 - k, 8), self.core]
            self.third[k] = remote(block, block, send3.at[k], recv3.at[k], lat, other, batch)

    def begin(self):
        for k in (4, 3, 5, 2, 6, 1, 7):
            self.first[k - 1].start()
        self.own.start()

    def middle(self):
        self.own.wait()
        for copy in self.first:
            copy.wait()
        for k in (3, 5, 1, 7, 4, 2, 6):
            self.second[k].start()
        self.third[0].start()

    def end(self, table, total):
        order = (0, 2, 6, 4, 1, 7, 3, 5)
        for i, k in enumerate(order):
            if i + 1 < 8:
                ahead = order[i + 1]
                self.second[ahead].wait()
                self.third[ahead].start()
            self.third[k].wait()
            at = lax.rem(self.q + 8 - k, 8)
            part = dot(table[at], self.cells[at].reshape(256, C))
            if i == 0:
                total[...] = part
            else:
                total[...] += part


def store_rows(parts, block, first):
    n, at = block.shape[0], 0
    while at < n:
        g, inside = divmod(first + at, 72)
        size = min(n - at, 72 - inside)
        parts[g // 16, (g // 4) % 4, g % 4, inside : inside + size, :] = block[at : at + size].astype(BF16)
        at += size


class Reduce:
    def __init__(self, x_first, parts, got1, acc1, got2, acc2, got3, blocks, got4, sems):
        s1, r1, s2, r2, s3, r3, s4, r4 = sems
        self.bufs = parts, got1, acc1, got2, acc2, got3, blocks, got4
        self.x_first = x_first
        lat, lon, batch = place()
        self.lat, self.core = lat, lax.rem(lon, 2)
        self.x = lon // 4
        self.y = lax.rem(lon // 2, 2) * 2 + batch
        core, x, y = self.core, self.x, self.y
        self.one = remote(parts.at[1 - core], got1, s1, r1, lat, lon + 1 - 2 * core, batch)

        def peer(along_x, k):
            if along_x:
                return lax.rem(x + k, 4), (lat, step(lon, 4 * k, NLON), batch)
            to = lax.rem(y + k, 4)
            return to, (lat, x * 4 + (to // 2) * 2 + core, lax.rem(to, 2))

        self.two, self.three = [], []
        for k in range(1, 4):
            to, device = peer(x_first, k)
            src = acc1.at[:, to] if x_first else acc1.at[to]
            self.two.append(remote(src, got2.at[k - 1], s2.at[k - 1], r2.at[k - 1], *device))
            to, device = peer(not x_first, k)
            self.three.append(remote(acc2.at[to], got3.at[k - 1], s3.at[k - 1], r3.at[k - 1], *device))
        to_lat = core * 4 + y
        self.is_own = to_lat == lat
        self.e_own = lax.rem(lon, 4) * 2 + batch
        self.four = [
            remote(blocks.at[e], got4.at[lat], s4.at[e], r4.at[lat], to_lat, x * 4 + e // 2, e % 2) for e in range(8)
        ]
        self.arrive = [remote(blocks.at[0], got4.at[h], s4.at[0], r4.at[h], to_lat, x * 4, 0) for h in range(8)]

    def swap_cores(self):
        self.one.start()

    def first_axis(self):
        parts, got1, acc1 = self.bufs[:3]
        self.one.wait()

        def add(i, _):
            for j in range(4):
                acc1[i, j] = (parts[self.core, i, j].astype(F32) + got1[i, j].astype(F32)).astype(BF16)
            return 0

        lax.fori_loop(0, 4, add, 0)
        for copy in self.two:
            copy.start()

    def second_axis(self):
        _, _, acc1, got2, acc2 = self.bufs[:5]
        for copy in self.two:
            copy.wait()
        for i in range(4):
            mine = acc1[i, self.x] if self.x_first else acc1[self.y, i]
            acc2[i] = (
                mine.astype(F32) + got2[0, i].astype(F32) + got2[1, i].astype(F32) + got2[2, i].astype(F32)
            ).astype(BF16)
        for copy in self.three:
            copy.start()

    def to_owners(self, with_mixing):
        _, _, _, _, acc2, got3, blocks, got4 = self.bufs
        for copy in self.three:
            copy.wait()
        mine = acc2[self.y if self.x_first else self.x]
        total = mine.astype(F32) + got3[0].astype(F32) + got3[1].astype(F32) + got3[2].astype(F32)
        for e in range(8):
            rows = [total[9 * e : 9 * e + 9], total[72 + e : 73 + e], jnp.zeros((6, C), F32)]
            blocks[e] = jnp.concatenate(rows, axis=0).astype(BF16)
        for e in range(8):
            mine = self.is_own & (self.e_own == e)

            @pl.when(jnp.logical_not(mine))
            def _():
                self.four[e].start()

            @pl.when(mine)
            def _():
                got4[self.lat] = blocks[e]

    def finish(self):
        got4 = self.bufs[-1]
        total = None
        for h in range(8):

            @pl.when(jnp.logical_not(self.is_own & (self.lat == h)))
            def _():
                self.arrive[h].wait_recv()

        for h in range(8):
            total = got4[h].astype(F32) if h == 0 else total + got4[h].astype(F32)
        for e in range(8):

            @pl.when(jnp.logical_not(self.is_own & (self.e_own == e)))
            def _():
                self.four[e].wait_send()

        return total


INPUTS = (
    "field", "cot", "dec", "sum8", "k0", "pool2", "k1", "pool4", "pick", "gain", "table", "synth", "mixing", "place",
    "up4", "up2", "up8",
)


def kernel(scales, n_in, *refs):
    src = dict(zip(INPUTS, refs[:n_in]))
    out_pred, out0, out1, outm, outg = refs[n_in : n_in + 5]
    names = [n for n in INPUTS if n != "field"]
    v = dict(zip(names, refs[n_in + 5 :]))
    (
        load_sem, ext, fs, x3, x3c, l0f, c1s, x13, level0, da0, level1, a1, p1, slot, gl2, edges, ring, halo_s, halo_r,
        edge_s, edge_r, halo_own, cells1, cells2, g1sem, g2sem, sc, coef, slot2, spec_own, level2, pred, pred_sem,
        g1s, slope, xg, gp0, red0, red1, gain_in, gain_got, gain_s, gain_r,
    ) = refs[n_in + 5 + len(names) :]
    cot, k0, k1, gain, table, mixing = (v[n] for n in ("cot", "k0", "k1", "gain", "table", "mixing"))
    lat, lon, batch = place()
    mode_owner = lat * NLON + lon
    base = pl.multiple_of(8 * (mode_owner // 2), 8)

    own = pltpu.make_async_copy(src["field"], ext.at[pl.ds(3, 16), pl.ds(16, 48)], halo_own)
    own.start()
    loads = {}
    for i, n in enumerate(names):
        ref = src[n].at[mode_owner] if n == "synth" else src[n]
        loads[n] = pltpu.make_async_copy(ref, v[n], load_sem.at[i])
        loads[n].start()
    n_peers = greet_all()
    pl.semaphore_wait(pltpu.get_barrier_semaphore(), n_peers)
    halo = halo_copies(src["field"], ext, halo_s, halo_r)
    for copy in halo:
        copy.start()

    for n in ("cot", "dec", "sum8"):
        loads[n].wait()
    for half in range(2):
        part = cot[8 * half : 8 * half + 8].reshape(384, C)
        a1[4 * half : 4 * half + 4] = dot(v["dec"][...], part).reshape(4, 32, C)
        gl2[8 * half : 8 * half + 8] = dot(v["sum8"][...], part)
    c1s[...] = jnp.zeros_like(c1s)
    g1s[...] = jnp.zeros_like(g1s)
    red0[0][:, :, :, 72:80, :] = jnp.zeros((2, 4, 4, 8, C), BF16)
    own.wait()
    fs[3:19, 16:64] = ext[3:19, 16:64].astype(F32)
    for n in ("k0", "pool2", "k1", "pool4", "pick"):
        loads[n].wait()
    for copy in halo:
        copy.wait()

    edge_top = lat == 0
    edge_bot = lat == NLAT - 1
    fs[3:19, 0:16] = ext[3:19, 0:16].astype(F32)
    fs[3:19, 64:80] = ext[3:19, 64:80].astype(F32)
    fs[0:3] = jnp.where(edge_top, 0.0, ext[0:3].astype(F32))
    fs[19:22] = jnp.where(edge_bot, 0.0, ext[19:22].astype(F32))
    for b in range(3):
        x3[:, :, b * C : (b + 1) * C] = fs[:, 7 + b : 71 + b, :].astype(BF16)

    def rows4(i, _):
        y = 4 * i
        acc = dot(x3[pl.ds(y, 4)].reshape(256, 3 * C), k0[0])
        acc += dot(x3[pl.ds(y + 1, 4)].reshape(256, 3 * C), k0[1])
        acc += dot(x3[pl.ds(y + 2, 4)].reshape(256, 3 * C), k0[2])
        act, grad = gelu_both(acc)
        out = fs[pl.ds(y + 1, 4), 8:72, :] + act.reshape(4, 64, C)
        l0f[pl.ds(y, 4)] = out.astype(BF16)
        level0[pl.ds(y, 4)] = out[:, 8:56].astype(BF16)
        da0[pl.ds(y, 4)] = grad.reshape(4, 64, C)[:, 8:56].astype(BF16)
        return 0

    lax.fori_loop(0, 5, rows4, 0)

    for y in range(10):
        row = dot(v["pool2"][...], l0f[2 * y : 2 * y + 2].reshape(128, C)).astype(BF16).astype(F32)
        if y == 0:
            row = jnp.where(edge_top, 0.0, row)
        if y == 9:
            row = jnp.where(edge_bot, 0.0, row)
        c1s[y, 8:40, :] = row
    for b in range(3):
        x13[:, :, b * C : (b + 1) * C] = c1s[:, 7 + b : 39 + b, :].astype(BF16)
    pre = dot(x13[0:8].reshape(256, 3 * C), k1[0])
    pre += dot(x13[1:9].reshape(256, 3 * C), k1[1])
    pre += dot(x13[2:10].reshape(256, 3 * C), k1[2])
    act, _ = gelu_both(pre)
    col = lax.broadcasted_iota(jnp.int32, (8, 32, C), 1)
    mine = (col >= 4) & (col < 28)
    p1[...] = jnp.where(mine, pre.reshape(8, 32, C), 0.0)
    lev1 = jnp.where(mine, c1s[1:9, 8:40, :] + act.reshape(8, 32, C), 0.0).astype(BF16)
    level1[...] = lev1
    for half in range(2):
        slot[8 * half : 8 * half + 8] = dot(v["pool4"][...], lev1[4 * half : 4 * half + 4].reshape(128, C)).astype(BF16)

    gather = Gather(slot, cells1, *g1sem)
    gather.begin()
    edges[:, 0] = dot(v["pick"][...], a1[...].reshape(256, C).astype(BF16)).astype(BF16).reshape(4, 16, C)
    edges[:, 1] = dot(v["pick"][...], p1[...].reshape(256, C).astype(BF16)).astype(BF16).reshape(4, 16, C)
    edge = edge_copies(edges, ring, edge_s, edge_r)
    for copy in edge:
        copy.start()
    for b in range(3):
        x3c[:, :, b * C : (b + 1) * C] = fs[2:20, 15 + b : 63 + b, :].astype(BF16)
    for n in ("gain", "table", "synth", "mixing", "place", "up4", "up2", "up8"):
        loads[n].wait()
    gather.middle()
    for copy in edge:
        copy.wait()
    g1s[:, 8:40, :] = dot(v["place"][...], ring[:, 0].reshape(160, C)).reshape(10, 32, C)
    g1s[1:9, 8:40, :] += a1[...]
    slope[...] = dot(v["place"][...], ring[:, 1].reshape(160, C)).reshape(10, 32, C)
    slope[1:9] += p1[...]
    _, grad1 = gelu_both(slope[...])
    slope[...] = grad1
    gather.end(table, sc)

    gr, gi = gain[:, :C], gain[:, C:]
    sr, si = sc[0:512], sc[512:1024]
    coef[0:512] = (gr * sr - gi * si).astype(BF16)
    coef[512:1024] = (gr * si + gi * sr).astype(BF16)
    filt = dot(v["synth"][8:24], coef[...]).astype(BF16)
    mixed = dot(filt, mixing[...])
    act, grad = gelu_both(mixed)
    cell = lax.rem(lax.broadcasted_iota(jnp.int32, (16, C), 0), 8)
    gm = jnp.where((cell >= 1) & (cell < 7), gl2[...] * grad, 0.0).astype(BF16)
    slot2[...] = dot_cols(gm, mixing[...]).astype(BF16)

    gather = Gather(slot2, cells2, *g2sem)
    gather.begin()
    level2[...] = (slot[...].astype(F32) + act).astype(BF16)
    mix = dot_rows(filt, gm)
    for g in range(32):
        red1[0][g // 16, (g // 4) % 4, g % 4, 72:80, :] = mix[8 * g : 8 * g + 8].astype(BF16)
    spec_own[:, :C] = sc[pl.ds(base, 8), :]
    spec_own[:, C:] = sc[pl.ds(512 + base, 8), :]

    def predict(r):
        low = dot(v["up2"][...], level1[r]) + dot(v["up8"][...], level2[8 * (r // 4) : 8 * (r // 4) + 8])
        high = level0[2 * r + 2 : 2 * r + 4].astype(F32) + low.reshape(2, 48, C)
        pred[2 * r : 2 * r + 2] = high.astype(BF16)

    for r in range(4):
        predict(r)
    gather.middle()
    for r in range(4, 8):
        predict(r)
    pred_out = pltpu.make_async_copy(pred, out_pred, pred_sem)
    pred_out.start()
    gather.end(table, sc)

    er, ei = sc[0:512], sc[512:1024]
    coef[0:512] = (gr * er + gi * ei).astype(BF16)
    coef[512:1024] = (gr * ei - gi * er).astype(BF16)
    back = dot(v["synth"][...], coef[...]).astype(BF16)
    gl1 = g1s[:, 8:40, :] + dot(v["up4"][...], back).reshape(10, 32, C)
    col = lax.broadcasted_iota(jnp.int32, (10, 32, C), 1)
    row = lax.broadcasted_iota(jnp.int32, (10, 32, C), 0)
    first = jnp.where(edge_top, 1, 0)
    last = jnp.where(edge_bot, 9, 10)
    valid = (col >= 3) & (col < 29) & (row >= first) & (row < last)
    gp1 = jnp.where(valid, gl1 * slope[...], 0.0)
    g1s[:, 8:40, :] = gp1
    gown = jnp.where((col[1:9] >= 4) & (col[1:9] < 28), gp1[1:9], 0.0).astype(BF16).reshape(256, C)
    for a in range(3):
        store_rows(red1[0], dot_rows(x13[a : a + 8].reshape(256, 3 * C), gown), 768 * a)
    sum1 = Reduce(False, *red1[:8], red1[8:])
    sum1.swap_cores()

    gc1 = gl1[1:9].reshape(256, C)
    for b in range(3):
        xg[...] = g1s[:, 7 + b : 39 + b, :].astype(BF16)
        for a in range(3):
            gc1 += dot_cols(xg[a : a + 8].reshape(256, C), k1[2 - a, (2 - b) * C : (3 - b) * C, :])
    high = gc1.astype(BF16)
    low = (gc1 - high.astype(F32)).astype(BF16)
    for r in range(8):
        up = dot(v["up2"][...], high[32 * r : 32 * r + 32]) + dot(v["up2"][...], low[32 * r : 32 * r + 32])
        gl0 = cot[2 * r : 2 * r + 2].astype(F32) + 0.25 * up.reshape(2, 48, C)
        gp0[2 * r : 2 * r + 2] = (gl0 * da0[2 * r + 2 : 2 * r + 4].astype(F32)).astype(BF16)
    sum1.first_axis()
    for a in range(3):
        store_rows(red0[0], dot_rows(x3c[a : a + 16].reshape(768, 3 * C), gp0[...].reshape(768, C)), 768 * a)
    sum0 = Reduce(True, *red0[:8], red0[8:])
    sum0.swap_cores()

    br, bi = sc[pl.ds(base, 8), :], sc[pl.ds(512 + base, 8), :]
    m = lax.rem(base + lax.broadcasted_iota(jnp.int32, (8, C), 0), 32)
    weight = jnp.where(m == 0, 1.0, 2.0)
    ar, ai = spec_own[:, :C], spec_own[:, C:]
    gain_in[:, :C] = weight * (ar * br + ai * bi)
    gain_in[:, C:] = weight * (ar * bi - ai * br)
    swap = remote(gain_in, gain_got, gain_s, gain_r, lat, lon, 1 - batch)
    swap.start()

    sum0.first_axis()
    sum1.second_axis()
    swap.wait()
    gain_in[...] = gain_in[...] + gain_got[...]
    for batch_at in range(2):
        for lon_at in range(2):

            @pl.when((batch == batch_at) & (lax.rem(lon, 2) == lon_at))
            def _():
                at = 4 * lon_at + 2 * batch_at
                for i in range(2):
                    for j in range(4):
                        outg[4 * i + j : 4 * i + j + 1, :] = gain_in[at + i : at + i + 1, 128 * j : 128 * j + 128]

    sum1.to_owners(True)
    sum0.second_axis()
    sum0.to_owners(False)
    t1 = sum1.finish()
    for r in range(9):
        for j in range(2):
            out1[2 * r + j : 2 * r + j + 1, :] = scales[1] * t1[r : r + 1, 128 * j : 128 * j + 128]
    for j in range(2):
        outm[j : j + 1, :] = scales[2] * t1[9:10, 128 * j : 128 * j + 128]
    t0 = sum0.finish()
    for r in range(9):
        for j in range(2):
            out0[2 * r + j : 2 * r + j + 1, :] = scales[0] * t0[r : r + 1, 128 * j : 128 * j + 128]
    pred_out.wait()


def dma(*n):
    return pltpu.SemaphoreType.DMA(n)


def vmem(*shape, dtype=BF16):
    return pltpu.VMEM(shape, dtype)


def reduce_scratch():
    return (
        vmem(2, 4, 4, 80, C), vmem(4, 4, 80, C), vmem(4, 4, 80, C), vmem(3, 4, 80, C), vmem(4, 80, C),
        vmem(3, 80, C), vmem(8, 16, C), vmem(8, 16, C),
        dma(), dma(), dma(3), dma(3), dma(3), dma(3), dma(8), dma(8),
    )


def on_device(tables, field, kernel0, kernel1, mixing, gain, cotangent):
    table, synth, small = tables
    args = {k: jnp.asarray(a) for k, a in small.items()}
    args |= dict(
        field=field[0], cot=cotangent[0], k0=kernel0.reshape(3, 3 * C, C), k1=kernel1.reshape(3, 3 * C, C),
        mixing=mixing, gain=gain, table=jnp.asarray(table), synth=jnp.asarray(synth),
    )
    cells0 = 2 * 128 * 768
    scales = (1.0 / math.sqrt(cells0), 1.0 / math.sqrt(cells0 // 4), 1.0 / math.sqrt(cells0 // 64))
    names = [n for n in INPUTS if n != "field"]
    gathers = (dma(), dma(7), dma(7), dma(7), dma(7), dma(8), dma(8))
    scratch = [vmem(32, 1024) if n == "synth" else vmem(*args[n].shape, dtype=args[n].dtype) for n in names]
    scratch += [
        dma(len(names)), vmem(22, 80, C), vmem(22, 80, C, dtype=F32), vmem(22, 64, 3 * C), vmem(18, 48, 3 * C),
        vmem(20, 64, C), vmem(10, 48, C, dtype=F32), vmem(10, 32, 3 * C), vmem(20, 48, C), vmem(20, 48, C),
        vmem(8, 32, C), vmem(8, 32, C, dtype=F32), vmem(8, 32, C, dtype=F32), vmem(16, C), vmem(16, C, dtype=F32),
        vmem(4, 2, 16, C), vmem(10, 2, 16, C), dma(8), dma(8), dma(8), dma(8), dma(),
        vmem(8, 2, 8, 16, C), vmem(8, 2, 8, 16, C), gathers, gathers, vmem(1024, C, dtype=F32), vmem(1024, C),
        vmem(16, C), vmem(8, 2 * C, dtype=F32), vmem(16, C), vmem(ROWS, COLS, C), dma(),
        vmem(10, 48, C, dtype=F32), vmem(10, 32, C, dtype=F32), vmem(10, 32, C), vmem(16, 48, C),
        reduce_scratch(), reduce_scratch(), vmem(8, 2 * C, dtype=F32), vmem(8, 2 * C, dtype=F32), dma(), dma(),
    ]
    anywhere = pl.BlockSpec(memory_space=pl.ANY)
    here = pl.BlockSpec(memory_space=pltpu.VMEM)
    predicted, grad0, grad1, gradm, gradg = pl.pallas_call(
        functools.partial(kernel, scales, len(INPUTS)),
        out_shape=[jax.ShapeDtypeStruct((ROWS, COLS, C), BF16)]
        + [jax.ShapeDtypeStruct((n, 128), F32) for n in (18, 18, 2, 8)],
        in_specs=[anywhere] * len(INPUTS),
        out_specs=[anywhere] + [here] * 4,
        scratch_shapes=scratch,
        compiler_params=pltpu.CompilerParams(collective_id=0, has_side_effects=True, vmem_limit_bytes=VMEM_BYTES),
    )(*[args[n] for n in INPUTS])
    return predicted[None], grad0.reshape(-1), grad1.reshape(-1), gradm.reshape(-1), gradg.reshape(-1)


def solution(mesh):
    tables = (*spectral_tables(), cell_tables())
    tile = P("batch", "lat", "lon", None)
    split = P(("lat", "lon", "batch"))
    return jax.shard_map(
        functools.partial(on_device, tables), mesh=mesh, in_specs=(tile, P(), P(), P(), P(), tile),
        out_specs=(tile, split, split, split, split), check_vma=False,
    )
```

time: 144 us -> 97.6 us (0.68)
  the two profiles are of different devices: /device:TPU:31 before, /device:TPU:1 now
where the time goes in v2:
time: 97.6 us; the launch traced here: 97.3 us
  Pallas kernels  89.8 us (92%)
  local copies, waits for them, and re-layouts  6.89 us (7%)
    pallas_call x1, Pallas kernels, on_device(): pl.pallas_call(functools.partial(kernel, scales, len(INPUTS)), out_shape=...  89.8 us
    unnamed x5, local copies, waits for them, and re-layouts  6.89 us

profile of v2, /device:TPU:1, one launch (start us, length us, event | category | flops | bytes accessed | tf_op | source)
XLA Modules:
  0.0 97.3 jit_solution(8704241978670119667)
XLA Ops:
  0.6 89.8 %shard_map.200 = (bf16[16,48,256]{2,1,0:T(8,128)(2,1)}, f32[18,128]{1,0:T(8,128)}, f32[18,128]{1,0:T(8,128)}, f32[2,128]{1,0:T(2,128)}, f32[8,128]{1,0:T(8,128)}) custom-call(bf16[16,48,256]{2,1,0:T(8,128)(2,1)} %bitcast.12, bf16[16,48,256]{2,1,0:T(8,128)(2,1)} %bitcast.13, bf16[128,384]{1,0:T(8,128)(2,1)} %constant.24.clone.refs_2_, ...), custom_call_target="tpu_custom_call" | custom-call | tf_op jit(solution)/shard_map/pallas_call | solution.py:617
  90.4 1.8 %copy.27 = bf16[1,16,48,256]{3,2,1,0:T(8,128)(2,1)} copy(bf16[1,16,48,256]{3,2,1,0:T(8,128)(2,1)} %bitcast.11) | data formatting | bytes 786432
  92.2 1.3 %copy.28 = f32[2304]{0:T(1024)} copy(f32[2304]{0:T(1024)} %bitcast.15) | data formatting | bytes 18432
  93.5 1.3 %copy.29 = f32[2304]{0:T(1024)} copy(f32[2304]{0:T(1024)} %bitcast.14) | data formatting | bytes 18432
  94.8 1.2 %copy.30 = f32[256]{0:T(256)} copy(f32[256]{0:T(256)} %bitcast.17) | data formatting | bytes 2048
  96.0 1.3 %copy.31 = f32[1024]{0:T(1024)} copy(f32[1024]{0:T(1024)} %bitcast.16) | data formatting | bytes 8192

commit v3 on v2

--- a/solution.py
+++ b/solution.py
@@ -93,7 +93,22 @@
     for j in range(48):
         up2[:, j, 4 + j // 2] = 1
         up8[:, j, 1 + j // 8] = 1
+    hpick = np.zeros((160, 16, 48))
+    hplace = np.zeros((22, 32, 160))
+    for j in range(3):
+        for r in range(16):
+            hpick[3 * r + j, r, j] = 1
+            hpick[48 + 3 * r + j, r, 45 + j] = 1
+            hplace[3 + r, 16 + j, 3 * r + j] = 1
+            hplace[3 + r, 13 + j, 48 + 3 * r + j] = 1
+        for i in range(3):
+            for seg, row, col, to_row, to_col in (
+                (96, 0, 0, 19, 16), (112, 0, 45, 19, 13), (128, 13, 0, 0, 16), (144, 13, 45, 0, 13)
+            ):
+                hpick[seg + 3 * i + j, row + i, col + j] = 1
+                hplace[to_row + i, to_col + j, seg + 3 * i + j] = 1
     shapes = dict(
+        hpick=(hpick, (160, 768)), hplace=(hplace, (704, 160)),
         pool2=(pool2, (32, 128)), pool4=(pool4, (8, 128)), dec=(dec, (128, 384)), sum8=(sum8, (8, 384)),
         pick=(pick, (64, 256)), place=(place, (320, 160)), up4=(up4, (320, 32)), up2=(up2, (96, 32)),
         up8=(up8, (96, 8)),
@@ -145,17 +160,20 @@
 NEIGHBOURS = ((1, 0), (-1, 0), (0, 1), (0, -1), (1, 1), (1, -1), (-1, 1), (-1, -1))
 
 
-def halo_copies(field, ext, send, recv):
+HALO_SENDS = (
+    ((0, -1), 0, 48), ((0, 1), 48, 48), ((-1, -1), 96, 16), ((-1, 1), 112, 16), ((1, -1), 128, 16), ((1, 1), 144, 16),
+)
+
+
+def halo_copies(field, rows_top, rows_bot, packed, halo, send, recv):
     lat, lon, batch = place()
-    rows = {1: (pl.ds(13, 3), pl.ds(0, 3)), -1: (pl.ds(0, 3), pl.ds(19, 3)), 0: (pl.ds(0, 16), pl.ds(3, 16))}
-    cols = {1: (pl.ds(32, 16), pl.ds(0, 16)), -1: (pl.ds(0, 16), pl.ds(64, 16)), 0: (pl.ds(0, 48), pl.ds(16, 48))}
-    copies = []
-    for i, (dlat, dlon) in enumerate(NEIGHBOURS):
-        (src_r, dst_r), (src_c, dst_c) = rows[dlat], cols[dlon]
-        copies.append(remote(
-            field.at[src_r, src_c], ext.at[dst_r, dst_c], send.at[i], recv.at[i],
-            step(lat, dlat, NLAT), step(lon, dlon, NLON), batch,
-        ))
+    copies = [
+        remote(packed.at[pl.ds(at, n)], halo.at[pl.ds(at, n)], send.at[i], recv.at[i],
+               step(lat, dlat, NLAT), step(lon, dlon, NLON), batch)
+        for i, ((dlat, dlon), at, n) in enumerate(HALO_SENDS)
+    ]
+    copies.append(remote(field.at[pl.ds(13, 3)], rows_top, send.at[6], recv.at[6], step(lat, 1, NLAT), lon, batch))
+    copies.append(remote(field.at[pl.ds(0, 3)], rows_bot, send.at[7], recv.at[7], step(lat, -1, NLAT), lon, batch))
     return copies
 
 
@@ -192,21 +210,29 @@
 
 
 class Gather:
-    def __init__(self, slot, cells, own, send1, recv1, send2, recv2, send3, recv3):
+    PAIRS = (0, 1, 3, 2)
+    FAR_FIRST = (3, 5, 1, 7, 4, 2, 6)
+    NEAR_FIRST = (0, 2, 6, 4, 1, 7, 3, 5)
+
+    def __init__(self, slot, cells, send1, recv1, send2, recv2, send3, recv3):
         lat, lon, batch = place()
-        self.q, self.core, self.cells = lon // 2, lax.rem(lon, 2), cells
+        self.q, self.core, self.cells, self.lat = lon // 2, lax.rem(lon, 2), cells, lat
         other = lon + 1 - 2 * self.core
         here = cells.at[self.q, self.core]
-        self.own = pltpu.make_async_copy(slot, here.at[lat], own)
+        self.own = pltpu.make_async_copy(slot, here.at[lat], recv1.at[lat])
         self.first = [
-            remote(slot, here.at[lat], send1.at[k - 1], recv1.at[k - 1], step(lat, k, NLAT), lon, batch)
+            remote(slot, here.at[lat], send1.at[k - 1], recv1.at[lat], step(lat, k, NLAT), lon, batch)
             for k in range(1, NLAT)
         ]
-        self.second = {
-            k: remote(here, here, send2.at[k - 1], recv2.at[k - 1], lat, step(lon, 2 * k, NLON), batch)
-            for k in range(1, 8)
-        }
-        self.third = {}
+        self.arrived = lambda l: pltpu.make_async_copy(slot, here.at[l], recv1.at[l])
+        self.second, self.third = {}, {}
+        for j, off in enumerate(self.PAIRS):
+            pair = pl.ds(2 * lax.rem(lat // 2 + off, 4), 2)
+            for k in range(1, 8):
+                self.second[k, j] = remote(
+                    here.at[pair], here.at[pair], send2.at[k - 1, j], recv2.at[k - 1, j],
+                    lat, step(lon, 2 * k, NLON), batch,
+                )
         for k in range(8):
             block = cells.at[lax.rem(self.q + 8 - k, 8), self.core]
             self.third[k] = remote(block, block, send3.at[k], recv3.at[k], lat, other, batch)
@@ -216,28 +242,33 @@
             self.first[k - 1].start()
         self.own.start()
 
-    def middle(self):
-        self.own.wait()
-        for copy in self.first:
-            copy.wait()
-        for k in (3, 5, 1, 7, 4, 2, 6):
-            self.second[k].start()
-        self.third[0].start()
+    def advance(self, j):
+        pair = lax.rem(self.lat // 2 + self.PAIRS[j], 4)
+        for i in range(2):
+            self.arrived(2 * pair + i).wait()
+        for k in self.FAR_FIRST:
+            self.second[k, j].start()
+        if j == 3:
+            self.third[0].start()
 
     def end(self, table, total):
-        order = (0, 2, 6, 4, 1, 7, 3, 5)
-        for i, k in enumerate(order):
+        for i, k in enumerate(self.NEAR_FIRST):
             if i + 1 < 8:
-                ahead = order[i + 1]
-                self.second[ahead].wait()
+                ahead = self.NEAR_FIRST[i + 1]
+                for j in range(4):
+                    self.second[ahead, j].wait_recv()
                 self.third[ahead].start()
-            self.third[k].wait()
+            self.third[k].wait_recv()
             at = lax.rem(self.q + 8 - k, 8)
             part = dot(table[at], self.cells[at].reshape(256, C))
             if i == 0:
                 total[...] = part
             else:
                 total[...] += part
+
+    def close(self):
+        for copy in [*self.first, *self.second.values(), *self.third.values()]:
+            copy.wait_send()
 
 
 def store_rows(parts, block, first):
@@ -351,7 +382,7 @@
 
 
 INPUTS = (
-    "field", "cot", "dec", "sum8", "k0", "pool2", "k1", "pool4", "pick", "gain", "table", "synth", "mixing", "place",
+    "field", "hpick", "cot", "dec", "sum8", "hplace", "k0", "pool2", "k1", "pool4", "pick", "gain", "table", "synth", "mixing", "place",
     "up4", "up2", "up8",
 )
 
@@ -359,28 +390,30 @@
 def kernel(scales, n_in, *refs):
     src = dict(zip(INPUTS, refs[:n_in]))
     out_pred, out0, out1, outm, outg = refs[n_in : n_in + 5]
-    names = [n for n in INPUTS if n != "field"]
+    names = list(INPUTS)
     v = dict(zip(names, refs[n_in + 5 :]))
     (
-        load_sem, ext, fs, x3, x3c, l0f, c1s, x13, level0, da0, level1, a1, p1, slot, gl2, edges, ring, halo_s, halo_r,
-        edge_s, edge_r, halo_own, cells1, cells2, g1sem, g2sem, sc, coef, slot2, spec_own, level2, pred, pred_sem,
+        load_sem, packed, halo_in, rows_top, rows_bot, fs, x3, x3c, l0f, c1s, x13, level0, da0, level1, a1, p1, slot, gl2, edges, ring, halo_s, halo_r,
+        edge_s, edge_r, cells1, cells2, g1sem, g2sem, sc, coef, slot2, spec_own, level2, pred, pred_sem,
         g1s, slope, xg, gp0, red0, red1, gain_in, gain_got, gain_s, gain_r,
     ) = refs[n_in + 5 + len(names) :]
     cot, k0, k1, gain, table, mixing = (v[n] for n in ("cot", "k0", "k1", "gain", "table", "mixing"))
+    field = v["field"]
     lat, lon, batch = place()
     mode_owner = lat * NLON + lon
     base = pl.multiple_of(8 * (mode_owner // 2), 8)
 
-    own = pltpu.make_async_copy(src["field"], ext.at[pl.ds(3, 16), pl.ds(16, 48)], halo_own)
-    own.start()
     loads = {}
     for i, n in enumerate(names):
         ref = src[n].at[mode_owner] if n == "synth" else src[n]
         loads[n] = pltpu.make_async_copy(ref, v[n], load_sem.at[i])
         loads[n].start()
     n_peers = greet_all()
+    loads["field"].wait()
+    loads["hpick"].wait()
+    packed[...] = dot(v["hpick"][...], field[...].reshape(768, C)).astype(BF16)
     pl.semaphore_wait(pltpu.get_barrier_semaphore(), n_peers)
-    halo = halo_copies(src["field"], ext, halo_s, halo_r)
+    halo = halo_copies(field, rows_top, rows_bot, packed, halo_in, halo_s, halo_r)
     for copy in halo:
         copy.start()
 
@@ -393,19 +426,21 @@
     c1s[...] = jnp.zeros_like(c1s)
     g1s[...] = jnp.zeros_like(g1s)
     red0[0][:, :, :, 72:80, :] = jnp.zeros((2, 4, 4, 8, C), BF16)
-    own.wait()
-    fs[3:19, 16:64] = ext[3:19, 16:64].astype(F32)
-    for n in ("k0", "pool2", "k1", "pool4", "pick"):
+    fs[3:19, 16:64] = field[...].astype(F32)
+    for n in ("hplace", "k0", "pool2", "k1", "pool4", "pick"):
         loads[n].wait()
     for copy in halo:
         copy.wait()
 
     edge_top = lat == 0
     edge_bot = lat == NLAT - 1
-    fs[3:19, 0:16] = ext[3:19, 0:16].astype(F32)
-    fs[3:19, 64:80] = ext[3:19, 64:80].astype(F32)
-    fs[0:3] = jnp.where(edge_top, 0.0, ext[0:3].astype(F32))
-    fs[19:22] = jnp.where(edge_bot, 0.0, ext[19:22].astype(F32))
+    fs[0:3, 16:64] = jnp.where(edge_top, 0.0, rows_top[...].astype(F32))
+    fs[19:22, 16:64] = jnp.where(edge_bot, 0.0, rows_bot[...].astype(F32))
+    sides = dot(v["hplace"][...], halo_in[...]).reshape(22, 32, C)
+    for half, at in ((0, 0), (16, 64)):
+        fs[0:3, at : at + 16] = jnp.where(edge_top, 0.0, sides[0:3, half : half + 16])
+        fs[3:19, at : at + 16] = sides[3:19, half : half + 16]
+        fs[19:22, at : at + 16] = jnp.where(edge_bot, 0.0, sides[19:22, half : half + 16])
     for b in range(3):
         x3[:, :, b * C : (b + 1) * C] = fs[:, 7 + b : 71 + b, :].astype(BF16)
 
@@ -451,11 +486,12 @@
     edge = edge_copies(edges, ring, edge_s, edge_r)
     for copy in edge:
         copy.start()
-    for b in range(3):
-        x3c[:, :, b * C : (b + 1) * C] = fs[2:20, 15 + b : 63 + b, :].astype(BF16)
     for n in ("gain", "table", "synth", "mixing", "place", "up4", "up2", "up8"):
         loads[n].wait()
-    gather.middle()
+    for b in range(3):
+        gather.advance(b)
+        x3c[:, :, b * C : (b + 1) * C] = fs[2:20, 15 + b : 63 + b, :].astype(BF16)
+    gather.advance(3)
     for copy in edge:
         copy.wait()
     g1s[:, 8:40, :] = dot(v["place"][...], ring[:, 0].reshape(160, C)).reshape(10, 32, C)
@@ -465,6 +501,7 @@
     _, grad1 = gelu_both(slope[...])
     slope[...] = grad1
     gather.end(table, sc)
+    first_gather = gather
 
     gr, gi = gain[:, :C], gain[:, C:]
     sr, si = sc[0:512], sc[512:1024]
@@ -491,11 +528,10 @@
         high = level0[2 * r + 2 : 2 * r + 4].astype(F32) + low.reshape(2, 48, C)
         pred[2 * r : 2 * r + 2] = high.astype(BF16)
 
-    for r in range(4):
-        predict(r)
-    gather.middle()
-    for r in range(4, 8):
-        predict(r)
+    for j in range(4):
+        gather.advance(j)
+        predict(2 * j)
+        predict(2 * j + 1)
     pred_out = pltpu.make_async_copy(pred, out_pred, pred_sem)
     pred_out.start()
     gather.end(table, sc)
@@ -571,6 +607,8 @@
     for r in range(9):
         for j in range(2):
             out0[2 * r + j : 2 * r + j + 1, :] = scales[0] * t0[r : r + 1, 128 * j : 128 * j + 128]
+    first_gather.close()
+    gather.close()
     pred_out.wait()
 
 
@@ -588,6 +626,28 @@
         vmem(3, 80, C), vmem(8, 16, C), vmem(8, 16, C),
         dma(), dma(), dma(3), dma(3), dma(3), dma(3), dma(8), dma(8),
     )
+
+
+def hand_over(*arrays):
+    n = len(arrays)
+
+    def body(*refs):
+        src, dst, buf, (come, go) = refs[:n], refs[n : 2 * n], refs[2 * n : 3 * n], refs[3 * n :]
+        inward = [pltpu.make_async_copy(src[i], buf[i], come.at[i]) for i in range(n)]
+        outward = [pltpu.make_async_copy(buf[i], dst[i], go.at[i]) for i in range(n)]
+        for copy in inward:
+            copy.start()
+        for i in range(n):
+            inward[i].wait()
+            outward[i].start()
+        for copy in outward:
+            copy.wait()
+
+    anywhere = pl.BlockSpec(memory_space=pl.ANY)
+    return pl.pallas_call(
+        body, out_shape=[jax.ShapeDtypeStruct(a.shape, a.dtype) for a in arrays], in_specs=[anywhere] * n,
+        out_specs=[anywhere] * n, scratch_shapes=[vmem(*a.shape, dtype=a.dtype) for a in arrays] + [dma(n), dma(n)],
+    )(*arrays)
 
 
 def on_device(tables, field, kernel0, kernel1, mixing, gain, cotangent):
@@ -599,14 +659,14 @@
     )
     cells0 = 2 * 128 * 768
     scales = (1.0 / math.sqrt(cells0), 1.0 / math.sqrt(cells0 // 4), 1.0 / math.sqrt(cells0 // 64))
-    names = [n for n in INPUTS if n != "field"]
-    gathers = (dma(), dma(7), dma(7), dma(7), dma(7), dma(8), dma(8))
+    names = INPUTS
+    gathers = (dma(7), dma(8), dma(7, 4), dma(7, 4), dma(8), dma(8))
     scratch = [vmem(32, 1024) if n == "synth" else vmem(*args[n].shape, dtype=args[n].dtype) for n in names]
     scratch += [
-        dma(len(names)), vmem(22, 80, C), vmem(22, 80, C, dtype=F32), vmem(22, 64, 3 * C), vmem(18, 48, 3 * C),
+        dma(len(names)), vmem(160, C), vmem(160, C), vmem(3, 48, C), vmem(3, 48, C), vmem(22, 80, C, dtype=F32), vmem(22, 64, 3 * C), vmem(18, 48, 3 * C),
         vmem(20, 64, C), vmem(10, 48, C, dtype=F32), vmem(10, 32, 3 * C), vmem(20, 48, C), vmem(20, 48, C),
         vmem(8, 32, C), vmem(8, 32, C, dtype=F32), vmem(8, 32, C, dtype=F32), vmem(16, C), vmem(16, C, dtype=F32),
-        vmem(4, 2, 16, C), vmem(10, 2, 16, C), dma(8), dma(8), dma(8), dma(8), dma(),
+        vmem(4, 2, 16, C), vmem(10, 2, 16, C), dma(8), dma(8), dma(8), dma(8),
         vmem(8, 2, 8, 16, C), vmem(8, 2, 8, 16, C), gathers, gathers, vmem(1024, C, dtype=F32), vmem(1024, C),
         vmem(16, C), vmem(8, 2 * C, dtype=F32), vmem(16, C), vmem(ROWS, COLS, C), dma(),
         vmem(10, 48, C, dtype=F32), vmem(10, 32, C, dtype=F32), vmem(10, 32, C), vmem(16, 48, C),
@@ -623,6 +683,7 @@
         scratch_shapes=scratch,
         compiler_params=pltpu.CompilerParams(collective_id=0, has_side_effects=True, vmem_limit_bytes=VMEM_BYTES),
     )(*[args[n] for n in INPUTS])
+    predicted, grad0, grad1, gradm, gradg = hand_over(predicted, grad0, grad1, gradm, gradg)
     return predicted[None], grad0.reshape(-1), grad1.reshape(-1), gradm.reshape(-1), gradg.reshape(-1)
 
 

time: 97.6 us -> 87.9 us (0.901)
  local copies, waits for them, and re-layouts: 6.89 us -> 0 us
  Pallas kernels: 89.8 us -> 87 us
    unnamed x5 -> x0, local copies, waits for them, and re-layouts: 6.89 us -> none
    pallas_call x1, Pallas kernels: 89.8 us -> 85.2 us  [on_device(): pl.pallas_call(functools.partial(kernel, scales, len(INPUTS)), out_shape=...]
    pallas_call x0 -> x1, Pallas kernels: none -> 1.84 us  [hand_over(): pl.pallas_call(body, out_shape=[jax.ShapeDtypeStruct(a.shape, a.dtype) fo...]
where the time goes in v3:
time: 87.9 us; the launch traced here: 87.6 us
  Pallas kernels  87 us (99%)
    pallas_call x1, Pallas kernels, on_device(): pl.pallas_call(functools.partial(kernel, scales, len(INPUTS)), out_shape=...  85.2 us
    pallas_call x1, Pallas kernels, hand_over(): pl.pallas_call(body, out_shape=[jax.ShapeDtypeStruct(a.shape, a.dtype) fo...  1.84 us

profile of v3, /device:TPU:1, one launch (start us, length us, event | category | flops | bytes accessed | tf_op | source)
XLA Modules:
  0.0 87.6 jit_solution(15011515429004487456)
XLA Ops:
  0.6 85.2 %shard_map.218 = (bf16[16,48,256]{2,1,0:T(8,128)(2,1)}, f32[18,128]{1,0:T(8,128)}, f32[18,128]{1,0:T(8,128)}, f32[2,128]{1,0:T(2,128)}, f32[8,128]{1,0:T(8,128)}) custom-call(bf16[16,48,256]{2,1,0:T(8,128)(2,1)} %bitcast.11, bf16[160,768]{1,0:T(8,128)(2,1)} %constant.26.clone.refs_1_, bf16[16,48,256]{2,1,0:T(8,128)(2,1)} %bitcast.12, ...), custom_call_target="tpu_custom_call" | custom-call | tf_op jit(solution)/shard_map/pallas_call | solution.py:677
  85.8 1.8 %shard_map.219 = (bf16[16,48,256]{2,1,0:T(8,128)(2,1)}, f32[18,128]{1,0:T(8,128)}, f32[18,128]{1,0:T(8,128)}, f32[2,128]{1,0:T(2,128)}, f32[8,128]{1,0:T(8,128)}) custom-call(bf16[16,48,256]{2,1,0:T(8,128)(2,1)} %get-tuple-element.15.refs_0_, f32[18,128]{1,0:T(8,128)} %get-tuple-element.16.refs_1_, f32[18,128]{1,0:T(8,128)} %get-tuple-element.17.refs_2_, ...), custom_call_target="tpu_custom_call" | custom-call | tf_op jit(solution)/shard_map/pallas_call | solution.py:647

commit v4 on v3

--- a/solution.py
+++ b/solution.py
@@ -271,26 +271,26 @@
             copy.wait_send()
 
 
-def store_rows(parts, block, first):
-    n, at = block.shape[0], 0
-    while at < n:
-        g, inside = divmod(first + at, 72)
-        size = min(n - at, 72 - inside)
-        parts[g // 16, (g // 4) % 4, g % 4, inside : inside + size, :] = block[at : at + size].astype(BF16)
-        at += size
+HALF = 1152
+
+
+PIECE = 384
 
 
 class Reduce:
-    def __init__(self, x_first, parts, got1, acc1, got2, acc2, got3, blocks, got4, sems):
+    def __init__(self, x_rows, out, got1, total1, acc1, got2x, got2y, acc2x, acc2y, got3x, got3y, blocks, got4, sems):
         s1, r1, s2, r2, s3, r3, s4, r4 = sems
-        self.bufs = parts, got1, acc1, got2, acc2, got3, blocks, got4
-        self.x_first = x_first
+        self.out, self.got1, self.total1, self.acc1 = out, got1, total1, acc1
+        self.blocks, self.got4 = blocks, got4
         lat, lon, batch = place()
         self.lat, self.core = lat, lax.rem(lon, 2)
         self.x = lon // 4
         self.y = lax.rem(lon // 2, 2) * 2 + batch
         core, x, y = self.core, self.x, self.y
-        self.one = remote(parts.at[1 - core], got1, s1, r1, lat, lon + 1 - 2 * core, batch)
+        self.one = []
+        for i, at in enumerate(range(0, out.shape[0], PIECE)):
+            part = pl.ds(at, min(PIECE, out.shape[0] - at))
+            self.one.append((part, remote(out.at[part], got1.at[part], s1.at[i], r1.at[i], lat, lon + 1 - 2 * core, batch)))
 
         def peer(along_x, k):
             if along_x:
@@ -298,55 +298,83 @@
             to = lax.rem(y + k, 4)
             return to, (lat, x * 4 + (to // 2) * 2 + core, lax.rem(to, 2))
 
-        self.two, self.three = [], []
-        for k in range(1, 4):
-            to, device = peer(x_first, k)
-            src = acc1.at[:, to] if x_first else acc1.at[to]
-            self.two.append(remote(src, got2.at[k - 1], s2.at[k - 1], r2.at[k - 1], *device))
-            to, device = peer(not x_first, k)
-            self.three.append(remote(acc2.at[to], got3.at[k - 1], s3.at[k - 1], r3.at[k - 1], *device))
-        to_lat = core * 4 + y
-        self.is_own = to_lat == lat
-        self.e_own = lax.rem(lon, 4) * 2 + batch
+        self.ways = []
+        for way, (rows, got2, acc2, got3) in enumerate((
+            (pl.ds(0, x_rows), got2x, acc2x, got3x), (pl.ds(x_rows, 80 - x_rows), got2y, acc2y, got3y)
+        )):
+            two, three = [], []
+            for k in (2, 1, 3):
+                to, device = peer(way == 0, k)
+                src = acc1.at[:, to, rows] if way == 0 else acc1.at[to, :, rows]
+                two.append(remote(src, got2.at[k - 1], s2.at[way, k - 1], r2.at[way, k - 1], *device))
+                to, device = peer(way == 1, k)
+                three.append(remote(acc2.at[to], got3.at[k - 1], s3.at[way, k - 1], r3.at[way, k - 1], *device))
+            self.ways.append((rows, got2, acc2, got3, two, three))
+        self.is_own = lat // 4 == core
+        self.e_own = lax.rem(lat, 4) * 2 + core
         self.four = [
-            remote(blocks.at[e], got4.at[lat], s4.at[e], r4.at[lat], to_lat, x * 4 + e // 2, e % 2) for e in range(8)
+            remote(blocks.at[e], got4.at[lat], s4.at[e], r4.at[lat], core * 4 + e // 2, lon - core + e % 2, batch)
+            for e in range(8)
         ]
-        self.arrive = [remote(blocks.at[0], got4.at[h], s4.at[0], r4.at[h], to_lat, x * 4, 0) for h in range(8)]
-
-    def swap_cores(self):
-        self.one.start()
+        self.arrive = [remote(blocks.at[0], got4.at[h], s4.at[0], r4.at[h], lat, lon + 1 - 2 * core, batch) for h in range(8)]
+
+    def halves(self, windows, grad):
+        n = grad.shape[0]
+        height = n // windows.shape[1]
+
+        def piece(i):
+            tap, side = i // 2, lax.rem(i, 2)
+            cols = pl.ds(pl.multiple_of(side * PIECE, 128), PIECE)
+            return dot_rows(windows[pl.ds(tap, height), :, cols].reshape(n, PIECE), grad)
+
+        for i in range(3):
+            self.out[PIECE * i : PIECE * i + PIECE, :] = piece(i + 3 - 3 * self.core).astype(BF16)
+            self.one[i][1].start()
+        for i in range(3):
+            self.total1[PIECE * i : PIECE * i + PIECE, :] = piece(i + 3 * self.core)
 
     def first_axis(self):
-        parts, got1, acc1 = self.bufs[:3]
-        self.one.wait()
-
-        def add(i, _):
-            for j in range(4):
-                acc1[i, j] = (parts[self.core, i, j].astype(F32) + got1[i, j].astype(F32)).astype(BF16)
-            return 0
-
-        lax.fori_loop(0, 4, add, 0)
-        for copy in self.two:
-            copy.start()
+        total1, acc1 = self.total1, self.acc1
+        for part, copy in self.one:
+            copy.wait_recv()
+            total1[part, :] += self.got1[part, :].astype(F32)
+        for x in range(4):
+            for y in range(4):
+                pieces = []
+                for e in range(8):
+                    w = x * 8 + (y // 2) * 4 + (e % 2) * 2 + y % 2
+                    at = 288 * (e // 2) + 9 * w
+                    pieces.append(total1[at : at + 9])
+                for e in range(8):
+                    w = x * 8 + (y // 2) * 4 + (e % 2) * 2 + y % 2
+                    at = HALF + 32 * (e // 2) + w
+                    pieces.append(total1[at : at + 1] if total1.shape[0] > HALF else jnp.zeros((1, C), F32))
+                acc1[y, x] = jnp.concatenate(pieces, axis=0).astype(BF16)
+        for i in range(3):
+            for way in range(2):
+                self.ways[way][4][i].start()
 
     def second_axis(self):
-        _, _, acc1, got2, acc2 = self.bufs[:5]
-        for copy in self.two:
-            copy.wait()
-        for i in range(4):
-            mine = acc1[i, self.x] if self.x_first else acc1[self.y, i]
-            acc2[i] = (
-                mine.astype(F32) + got2[0, i].astype(F32) + got2[1, i].astype(F32) + got2[2, i].astype(F32)
-            ).astype(BF16)
-        for copy in self.three:
-            copy.start()
-
-    def to_owners(self, with_mixing):
-        _, _, _, _, acc2, got3, blocks, got4 = self.bufs
-        for copy in self.three:
-            copy.wait()
-        mine = acc2[self.y if self.x_first else self.x]
-        total = mine.astype(F32) + got3[0].astype(F32) + got3[1].astype(F32) + got3[2].astype(F32)
+        for way, (rows, got2, acc2, _, two, three) in enumerate(self.ways):
+            for copy in two:
+                copy.wait_recv()
+            for i in range(4):
+                mine = self.acc1[i, self.x, rows] if way == 0 else self.acc1[self.y, i, rows]
+                acc2[i] = (
+                    mine.astype(F32) + got2[0, i].astype(F32) + got2[1, i].astype(F32) + got2[2, i].astype(F32)
+                ).astype(BF16)
+            for copy in three:
+                copy.start()
+
+    def to_owners(self):
+        blocks, got4 = self.blocks, self.got4
+        totals = []
+        for way, (_, _, acc2, got3, _, three) in enumerate(self.ways):
+            for copy in three:
+                copy.wait_recv()
+            mine = acc2[self.y if way == 0 else self.x]
+            totals.append(mine.astype(F32) + got3[0].astype(F32) + got3[1].astype(F32) + got3[2].astype(F32))
+        total = jnp.concatenate(totals, axis=0)
         for e in range(8):
             rows = [total[9 * e : 9 * e + 9], total[72 + e : 73 + e], jnp.zeros((6, C), F32)]
             blocks[e] = jnp.concatenate(rows, axis=0).astype(BF16)
@@ -362,7 +390,7 @@
                 got4[self.lat] = blocks[e]
 
     def finish(self):
-        got4 = self.bufs[-1]
+        got4 = self.got4
         total = None
         for h in range(8):
 
@@ -378,6 +406,8 @@
             def _():
                 self.four[e].wait_send()
 
+        for copy in [c for _, c in self.one] + [c for way in self.ways for c in way[4] + way[5]]:
+            copy.wait_send()
         return total
 
 
@@ -395,7 +425,7 @@
     (
         load_sem, packed, halo_in, rows_top, rows_bot, fs, x3, x3c, l0f, c1s, x13, level0, da0, level1, a1, p1, slot, gl2, edges, ring, halo_s, halo_r,
         edge_s, edge_r, cells1, cells2, g1sem, g2sem, sc, coef, slot2, spec_own, level2, pred, pred_sem,
-        g1s, slope, xg, gp0, red0, red1, gain_in, gain_got, gain_s, gain_r,
+        g1s, slope, xg, gp0, mixes, red0, red1, gain_in, gain_got, gain_s, gain_r,
     ) = refs[n_in + 5 + len(names) :]
     cot, k0, k1, gain, table, mixing = (v[n] for n in ("cot", "k0", "k1", "gain", "table", "mixing"))
     field = v["field"]
@@ -403,12 +433,14 @@
     mode_owner = lat * NLON + lon
     base = pl.multiple_of(8 * (mode_owner // 2), 8)
 
+    n_peers = greet_all()
     loads = {}
     for i, n in enumerate(names):
         ref = src[n].at[mode_owner] if n == "synth" else src[n]
         loads[n] = pltpu.make_async_copy(ref, v[n], load_sem.at[i])
+    early = ("field", "hpick", "cot", "dec", "sum8")
+    for n in early:
         loads[n].start()
-    n_peers = greet_all()
     loads["field"].wait()
     loads["hpick"].wait()
     packed[...] = dot(v["hpick"][...], field[...].reshape(768, C)).astype(BF16)
@@ -416,6 +448,9 @@
     halo = halo_copies(field, rows_top, rows_bot, packed, halo_in, halo_s, halo_r)
     for copy in halo:
         copy.start()
+    for n in names:
+        if n not in early:
+            loads[n].start()
 
     for n in ("cot", "dec", "sum8"):
         loads[n].wait()
@@ -425,7 +460,6 @@
         gl2[8 * half : 8 * half + 8] = dot(v["sum8"][...], part)
     c1s[...] = jnp.zeros_like(c1s)
     g1s[...] = jnp.zeros_like(g1s)
-    red0[0][:, :, :, 72:80, :] = jnp.zeros((2, 4, 4, 8, C), BF16)
     fs[3:19, 16:64] = field[...].astype(F32)
     for n in ("hplace", "k0", "pool2", "k1", "pool4", "pick"):
         loads[n].wait()
@@ -514,12 +548,16 @@
     gm = jnp.where((cell >= 1) & (cell < 7), gl2[...] * grad, 0.0).astype(BF16)
     slot2[...] = dot_cols(gm, mixing[...]).astype(BF16)
 
+    sum1 = Reduce(32, *red1[:12], red1[12:])
+    sum0 = Reduce(48, *red0[:12], red0[12:])
+
     gather = Gather(slot2, cells2, *g2sem)
     gather.begin()
     level2[...] = (slot[...].astype(F32) + act).astype(BF16)
     mix = dot_rows(filt, gm)
-    for g in range(32):
-        red1[0][g // 16, (g // 4) % 4, g % 4, 72:80, :] = mix[8 * g : 8 * g + 8].astype(BF16)
+    mixes[...] = mix
+    sum1.out[HALF : HALF + 128, :] = mixes[pl.ds(pl.multiple_of(128 - 128 * sum1.core, 128), 128), :].astype(BF16)
+    sum1.total1[HALF : HALF + 128, :] = mixes[pl.ds(pl.multiple_of(128 * sum1.core, 128), 128), :]
     spec_own[:, :C] = sc[pl.ds(base, 8), :]
     spec_own[:, C:] = sc[pl.ds(512 + base, 8), :]
 
@@ -549,10 +587,8 @@
     gp1 = jnp.where(valid, gl1 * slope[...], 0.0)
     g1s[:, 8:40, :] = gp1
     gown = jnp.where((col[1:9] >= 4) & (col[1:9] < 28), gp1[1:9], 0.0).astype(BF16).reshape(256, C)
-    for a in range(3):
-        store_rows(red1[0], dot_rows(x13[a : a + 8].reshape(256, 3 * C), gown), 768 * a)
-    sum1 = Reduce(False, *red1[:8], red1[8:])
-    sum1.swap_cores()
+    sum1.halves(x13, gown)
+    sum1.one[3][1].start()
 
     gc1 = gl1[1:9].reshape(256, C)
     for b in range(3):
@@ -566,10 +602,7 @@
         gl0 = cot[2 * r : 2 * r + 2].astype(F32) + 0.25 * up.reshape(2, 48, C)
         gp0[2 * r : 2 * r + 2] = (gl0 * da0[2 * r + 2 : 2 * r + 4].astype(F32)).astype(BF16)
     sum1.first_axis()
-    for a in range(3):
-        store_rows(red0[0], dot_rows(x3c[a : a + 16].reshape(768, 3 * C), gp0[...].reshape(768, C)), 768 * a)
-    sum0 = Reduce(True, *red0[:8], red0[8:])
-    sum0.swap_cores()
+    sum0.halves(x3c, gp0[...].reshape(768, C))
 
     br, bi = sc[pl.ds(base, 8), :], sc[pl.ds(512 + base, 8), :]
     m = lax.rem(base + lax.broadcasted_iota(jnp.int32, (8, C), 0), 32)
@@ -594,9 +627,9 @@
                     for j in range(4):
                         outg[4 * i + j : 4 * i + j + 1, :] = gain_in[at + i : at + i + 1, 128 * j : 128 * j + 128]
 
-    sum1.to_owners(True)
+    sum1.to_owners()
     sum0.second_axis()
-    sum0.to_owners(False)
+    sum0.to_owners()
     t1 = sum1.finish()
     for r in range(9):
         for j in range(2):
@@ -620,11 +653,13 @@
     return pltpu.VMEM(shape, dtype)
 
 
-def reduce_scratch():
+def reduce_scratch(rows, x_rows):
+    y_rows = 80 - x_rows
     return (
-        vmem(2, 4, 4, 80, C), vmem(4, 4, 80, C), vmem(4, 4, 80, C), vmem(3, 4, 80, C), vmem(4, 80, C),
-        vmem(3, 80, C), vmem(8, 16, C), vmem(8, 16, C),
-        dma(), dma(), dma(3), dma(3), dma(3), dma(3), dma(8), dma(8),
+        vmem(rows, C), vmem(rows, C), vmem(rows, C, dtype=F32), vmem(4, 4, 80, C),
+        vmem(3, 4, x_rows, C), vmem(3, 4, y_rows, C), vmem(4, x_rows, C), vmem(4, y_rows, C),
+        vmem(3, x_rows, C), vmem(3, y_rows, C), vmem(8, 16, C), vmem(8, 16, C),
+        dma(4), dma(4), dma(2, 3), dma(2, 3), dma(2, 3), dma(2, 3), dma(8), dma(8),
     )
 
 
@@ -670,7 +705,7 @@
         vmem(8, 2, 8, 16, C), vmem(8, 2, 8, 16, C), gathers, gathers, vmem(1024, C, dtype=F32), vmem(1024, C),
         vmem(16, C), vmem(8, 2 * C, dtype=F32), vmem(16, C), vmem(ROWS, COLS, C), dma(),
         vmem(10, 48, C, dtype=F32), vmem(10, 32, C, dtype=F32), vmem(10, 32, C), vmem(16, 48, C),
-        reduce_scratch(), reduce_scratch(), vmem(8, 2 * C, dtype=F32), vmem(8, 2 * C, dtype=F32), dma(), dma(),
+        vmem(C, C, dtype=F32), reduce_scratch(HALF, 48), reduce_scratch(HALF + 128, 32), vmem(8, 2 * C, dtype=F32), vmem(8, 2 * C, dtype=F32), dma(), dma(),
     ]
     anywhere = pl.BlockSpec(memory_space=pl.ANY)
     here = pl.BlockSpec(memory_space=pltpu.VMEM)

time: 87.9 us -> 81.8 us (0.931)
  Pallas kernels: 87 us -> 81.1 us
    pallas_call x1, Pallas kernels: 85.2 us -> 79.2 us  [on_device(): pl.pallas_call(functools.partial(kernel, scales, len(INPUTS)), out_shape=...]
where the time goes in v4:
time: 81.8 us; the launch traced here: 81.7 us
  Pallas kernels  81.1 us (99%)
    pallas_call x1, Pallas kernels, on_device(): pl.pallas_call(functools.partial(kernel, scales, len(INPUTS)), out_shape=...  79.2 us
    pallas_call x1, Pallas kernels, hand_over(): pl.pallas_call(body, out_shape=[jax.ShapeDtypeStruct(a.shape, a.dtype) fo...  1.84 us

profile of v4, /device:TPU:1, one launch (start us, length us, event | category | flops | bytes accessed | tf_op | source)
XLA Modules:
  0.0 81.7 jit_solution(68190677543271508)
XLA Ops:
  0.6 79.2 %shard_map.218 = (bf16[16,48,256]{2,1,0:T(8,128)(2,1)}, f32[18,128]{1,0:T(8,128)}, f32[18,128]{1,0:T(8,128)}, f32[2,128]{1,0:T(2,128)}, f32[8,128]{1,0:T(8,128)}) custom-call(bf16[16,48,256]{2,1,0:T(8,128)(2,1)} %bitcast.11, bf16[160,768]{1,0:T(8,128)(2,1)} %constant.26.clone.refs_1_, bf16[16,48,256]{2,1,0:T(8,128)(2,1)} %bitcast.12, ...), custom_call_target="tpu_custom_call" | custom-call | tf_op jit(solution)/shard_map/pallas_call | solution.py:712
  79.9 1.8 %shard_map.219 = (bf16[16,48,256]{2,1,0:T(8,128)(2,1)}, f32[18,128]{1,0:T(8,128)}, f32[18,128]{1,0:T(8,128)}, f32[2,128]{1,0:T(2,128)}, f32[8,128]{1,0:T(8,128)}) custom-call(bf16[16,48,256]{2,1,0:T(8,128)(2,1)} %get-tuple-element.15.refs_0_, f32[18,128]{1,0:T(8,128)} %get-tuple-element.16.refs_1_, f32[18,128]{1,0:T(8,128)} %get-tuple-element.17.refs_2_, ...), custom_call_target="tpu_custom_call" | custom-call | tf_op jit(solution)/shard_map/pallas_call | solution.py:682

commit v5 on v4

--- a/solution.py
+++ b/solution.py
@@ -42,13 +42,13 @@
     back = np.zeros((NLAT * NLON, 32, 2, kl * km))
     for lat in range(NLAT):
         for lon in range(NLON):
-            i = np.repeat(lat * 2 - 1 + np.arange(4), 8)
+            i = np.repeat(lat * 2 + np.array([0, 1, -1, 2]), 8)
             j = np.tile(lon * 6 - 1 + np.arange(8), 4)
             ph = phase(i, j).T
             back[lat * NLON + lon, :, 0] = np.cos(ph) * weight
             back[lat * NLON + lon, :, 1] = -np.sin(ph) * weight
-    back = back.reshape(NLAT * NLON, 32, 2 * kl * km)
-    forward = forward.reshape(2 * kl * km, 8, 256).transpose(1, 0, 2)
+    back = back.reshape(NLAT, NLON, 32, 2 * kl * km)
+    forward = forward.reshape(2 * kl * km, NLON, NLAT * 16).transpose(1, 0, 2)
     return forward.astype(ml_dtypes.bfloat16), back.astype(ml_dtypes.bfloat16)
 
 
@@ -87,7 +87,7 @@
     up4 = np.zeros((10, 32, 4, 8))
     for r in range(10):
         for j in range(32):
-            up4[r, j, (r + 3) // 4, j // 4] = 1 / 16
+            up4[r, j, (2, 0, 1, 3)[(r + 3) // 4], j // 4] = 1 / 16
     up2 = np.zeros((2, 48, 32))
     up8 = np.zeros((2, 48, 8))
     for j in range(48):
@@ -198,76 +198,79 @@
     lat, lon, batch = place()
     for k in range(1, NLAT):
         signal(step(lat, k, NLAT), lon, batch)
-    for k in (1, -1):
+    for k in range(1, NLON):
         signal(lat, step(lon, k, NLON), batch)
     for dlat, dlon in NEIGHBOURS[4:]:
         signal(step(lat, dlat, NLAT), step(lon, dlon, NLON), batch)
-    for k in range(1, 8):
-        signal(lat, step(lon, 2 * k, NLON), batch)
     signal(lat, lon, 1 - batch)
     signal(lat, lon + 2 - 4 * lax.rem(lon // 2, 2), 1 - batch)
-    return 22
-
-
-class Gather:
-    PAIRS = (0, 1, 3, 2)
-    FAR_FIRST = (3, 5, 1, 7, 4, 2, 6)
-    NEAR_FIRST = (0, 2, 6, 4, 1, 7, 3, 5)
-
-    def __init__(self, slot, cells, send1, recv1, send2, recv2, send3, recv3):
+    return 28
+
+
+class Spectral:
+    FAR_FIRST = (10, 6, 9, 7, 11, 5, 8, 12, 4, 3, 13, 2, 14, 1, 15)
+
+    def __init__(self, slot, cells, share, got, modes, got_modes, send1, recv1, send2, recv2, send3, recv3):
         lat, lon, batch = place()
-        self.q, self.core, self.cells, self.lat = lon // 2, lax.rem(lon, 2), cells, lat
-        other = lon + 1 - 2 * self.core
-        here = cells.at[self.q, self.core]
-        self.own = pltpu.make_async_copy(slot, here.at[lat], recv1.at[lat])
+        self.lat, self.lon, self.cells = lat, lon, cells
+        self.share, self.got, self.modes, self.got_modes = share, got, modes, got_modes
+        self.own = pltpu.make_async_copy(slot, cells.at[lat], recv1.at[lat])
         self.first = [
-            remote(slot, here.at[lat], send1.at[k - 1], recv1.at[lat], step(lat, k, NLAT), lon, batch)
+            remote(slot, cells.at[lat], send1.at[k - 1], recv1.at[lat], step(lat, k, NLAT), lon, batch)
             for k in range(1, NLAT)
         ]
-        self.arrived = lambda l: pltpu.make_async_copy(slot, here.at[l], recv1.at[l])
-        self.second, self.third = {}, {}
-        for j, off in enumerate(self.PAIRS):
-            pair = pl.ds(2 * lax.rem(lat // 2 + off, 4), 2)
-            for k in range(1, 8):
-                self.second[k, j] = remote(
-                    here.at[pair], here.at[pair], send2.at[k - 1, j], recv2.at[k - 1, j],
-                    lat, step(lon, 2 * k, NLON), batch,
-                )
-        for k in range(8):
-            block = cells.at[lax.rem(self.q + 8 - k, 8), self.core]
-            self.third[k] = remote(block, block, send3.at[k], recv3.at[k], lat, other, batch)
+        self.arrived = [pltpu.make_async_copy(slot, cells.at[l], recv1.at[l]) for l in range(NLAT)]
+        self.second, self.third = [], []
+        for k in self.FAR_FIRST:
+            to = step(lon, k, NLON)
+            self.second.append(remote(share.at[to], got.at[lon], send2.at[k - 1], recv2.at[k - 1], lat, to, batch))
+            self.third.append(remote(modes.at[to], got_modes.at[lon], send3.at[k - 1], recv3.at[k - 1], lat, to, batch))
 
     def begin(self):
         for k in (4, 3, 5, 2, 6, 1, 7):
             self.first[k - 1].start()
         self.own.start()
 
-    def advance(self, j):
-        pair = lax.rem(self.lat // 2 + self.PAIRS[j], 4)
-        for i in range(2):
-            self.arrived(2 * pair + i).wait()
-        for k in self.FAR_FIRST:
-            self.second[k, j].start()
-        if j == 3:
-            self.third[0].start()
-
-    def end(self, table, total):
-        for i, k in enumerate(self.NEAR_FIRST):
-            if i + 1 < 8:
-                ahead = self.NEAR_FIRST[i + 1]
-                for j in range(4):
-                    self.second[ahead, j].wait_recv()
-                self.third[ahead].start()
-            self.third[k].wait_recv()
-            at = lax.rem(self.q + 8 - k, 8)
-            part = dot(table[at], self.cells[at].reshape(256, C))
-            if i == 0:
-                total[...] = part
-            else:
-                total[...] += part
+    def spread(self, table, gain, sign, synth, sc, coef):
+        for copy in self.arrived:
+            copy.wait()
+        sc[...] = dot(table[...], self.cells[...].reshape(NLAT * 16, C))
+        gr, gi = gain[:, :C], gain[:, C:] * sign
+        sr, si = sc[0:512], sc[512:1024]
+        coef[0:512] = (gr * sr - gi * si).astype(BF16)
+        coef[512:1024] = (gr * si + gi * sr).astype(BF16)
+        rows = self.share.shape[1]
+        weights = synth[:, 0:rows].reshape(NLON * rows, 1024)
+        self.share[...] = dot(weights, coef[...]).astype(BF16).reshape(NLON, rows, C)
+        for copy in self.second:
+            copy.start()
+        self.got[self.lon] = self.share[self.lon]
+        re = sc[pl.ds(pl.multiple_of(64 * self.lat, 8), 64), :]
+        im = sc[pl.ds(pl.multiple_of(512 + 64 * self.lat, 8), 64), :]
+        for to in range(NLON):
+            self.modes[to] = jnp.concatenate([re[4 * to : 4 * to + 4], im[4 * to : 4 * to + 4]], axis=0)
+        for copy in self.third:
+            copy.start()
+        self.got_modes[self.lon] = self.modes[self.lon]
+
+    def collect(self):
+        for copy in self.second:
+            copy.wait_recv()
+        total = self.got[0].astype(F32)
+        for h in range(1, NLON):
+            total += self.got[h].astype(F32)
+        return total.astype(BF16)
+
+    def collect_modes(self):
+        for copy in self.third:
+            copy.wait_recv()
+        total = self.got_modes[0]
+        for h in range(1, NLON):
+            total += self.got_modes[h]
+        return total
 
     def close(self):
-        for copy in [*self.first, *self.second.values(), *self.third.values()]:
+        for copy in self.first + self.second + self.third:
             copy.wait_send()
 
 
@@ -424,19 +427,17 @@
     v = dict(zip(names, refs[n_in + 5 :]))
     (
         load_sem, packed, halo_in, rows_top, rows_bot, fs, x3, x3c, l0f, c1s, x13, level0, da0, level1, a1, p1, slot, gl2, edges, ring, halo_s, halo_r,
-        edge_s, edge_r, cells1, cells2, g1sem, g2sem, sc, coef, slot2, spec_own, level2, pred, pred_sem,
+        edge_s, edge_r, spec1, spec2, sc, coef, slot2, level2, pred, pred_sem,
         g1s, slope, xg, gp0, mixes, red0, red1, gain_in, gain_got, gain_s, gain_r,
     ) = refs[n_in + 5 + len(names) :]
     cot, k0, k1, gain, table, mixing = (v[n] for n in ("cot", "k0", "k1", "gain", "table", "mixing"))
     field = v["field"]
     lat, lon, batch = place()
-    mode_owner = lat * NLON + lon
-    base = pl.multiple_of(8 * (mode_owner // 2), 8)
 
     n_peers = greet_all()
     loads = {}
     for i, n in enumerate(names):
-        ref = src[n].at[mode_owner] if n == "synth" else src[n]
+        ref = src[n].at[dict(synth=lat, table=lon)[n]] if n in ("synth", "table") else src[n]
         loads[n] = pltpu.make_async_copy(ref, v[n], load_sem.at[i])
     early = ("field", "hpick", "cot", "dec", "sum8")
     for n in early:
@@ -513,8 +514,8 @@
     for half in range(2):
         slot[8 * half : 8 * half + 8] = dot(v["pool4"][...], lev1[4 * half : 4 * half + 4].reshape(128, C)).astype(BF16)
 
-    gather = Gather(slot, cells1, *g1sem)
-    gather.begin()
+    forth = Spectral(slot, *spec1[:5], *spec1[5:])
+    forth.begin()
     edges[:, 0] = dot(v["pick"][...], a1[...].reshape(256, C).astype(BF16)).astype(BF16).reshape(4, 16, C)
     edges[:, 1] = dot(v["pick"][...], p1[...].reshape(256, C).astype(BF16)).astype(BF16).reshape(4, 16, C)
     edge = edge_copies(edges, ring, edge_s, edge_r)
@@ -523,9 +524,8 @@
     for n in ("gain", "table", "synth", "mixing", "place", "up4", "up2", "up8"):
         loads[n].wait()
     for b in range(3):
-        gather.advance(b)
         x3c[:, :, b * C : (b + 1) * C] = fs[2:20, 15 + b : 63 + b, :].astype(BF16)
-    gather.advance(3)
+    forth.spread(table, gain, 1.0, v["synth"], sc, coef)
     for copy in edge:
         copy.wait()
     g1s[:, 8:40, :] = dot(v["place"][...], ring[:, 0].reshape(160, C)).reshape(10, 32, C)
@@ -534,14 +534,7 @@
     slope[1:9] += p1[...]
     _, grad1 = gelu_both(slope[...])
     slope[...] = grad1
-    gather.end(table, sc)
-    first_gather = gather
-
-    gr, gi = gain[:, :C], gain[:, C:]
-    sr, si = sc[0:512], sc[512:1024]
-    coef[0:512] = (gr * sr - gi * si).astype(BF16)
-    coef[512:1024] = (gr * si + gi * sr).astype(BF16)
-    filt = dot(v["synth"][8:24], coef[...]).astype(BF16)
+    filt = forth.collect()
     mixed = dot(filt, mixing[...])
     act, grad = gelu_both(mixed)
     cell = lax.rem(lax.broadcasted_iota(jnp.int32, (16, C), 0), 8)
@@ -551,33 +544,29 @@
     sum1 = Reduce(32, *red1[:12], red1[12:])
     sum0 = Reduce(48, *red0[:12], red0[12:])
 
-    gather = Gather(slot2, cells2, *g2sem)
-    gather.begin()
+    back_way = Spectral(slot2, *spec2[:5], *spec2[5:])
+    back_way.begin()
     level2[...] = (slot[...].astype(F32) + act).astype(BF16)
     mix = dot_rows(filt, gm)
     mixes[...] = mix
     sum1.out[HALF : HALF + 128, :] = mixes[pl.ds(pl.multiple_of(128 - 128 * sum1.core, 128), 128), :].astype(BF16)
     sum1.total1[HALF : HALF + 128, :] = mixes[pl.ds(pl.multiple_of(128 * sum1.core, 128), 128), :]
-    spec_own[:, :C] = sc[pl.ds(base, 8), :]
-    spec_own[:, C:] = sc[pl.ds(512 + base, 8), :]
+    spec_own = forth.collect_modes()
 
     def predict(r):
         low = dot(v["up2"][...], level1[r]) + dot(v["up8"][...], level2[8 * (r // 4) : 8 * (r // 4) + 8])
         high = level0[2 * r + 2 : 2 * r + 4].astype(F32) + low.reshape(2, 48, C)
         pred[2 * r : 2 * r + 2] = high.astype(BF16)
 
-    for j in range(4):
-        gather.advance(j)
-        predict(2 * j)
-        predict(2 * j + 1)
+    for r in range(4):
+        predict(r)
+    back_way.spread(table, gain, -1.0, v["synth"], sc, coef)
+    for r in range(4, 8):
+        predict(r)
     pred_out = pltpu.make_async_copy(pred, out_pred, pred_sem)
     pred_out.start()
-    gather.end(table, sc)
-
-    er, ei = sc[0:512], sc[512:1024]
-    coef[0:512] = (gr * er + gi * ei).astype(BF16)
-    coef[512:1024] = (gr * ei - gi * er).astype(BF16)
-    back = dot(v["synth"][...], coef[...]).astype(BF16)
+
+    back = back_way.collect()
     gl1 = g1s[:, 8:40, :] + dot(v["up4"][...], back).reshape(10, 32, C)
     col = lax.broadcasted_iota(jnp.int32, (10, 32, C), 1)
     row = lax.broadcasted_iota(jnp.int32, (10, 32, C), 0)
@@ -604,12 +593,13 @@
     sum1.first_axis()
     sum0.halves(x3c, gp0[...].reshape(768, C))
 
-    br, bi = sc[pl.ds(base, 8), :], sc[pl.ds(512 + base, 8), :]
-    m = lax.rem(base + lax.broadcasted_iota(jnp.int32, (8, C), 0), 32)
+    grads = back_way.collect_modes()
+    m = lax.rem(4 * lon + lax.broadcasted_iota(jnp.int32, (4, C), 0), 32)
     weight = jnp.where(m == 0, 1.0, 2.0)
-    ar, ai = spec_own[:, :C], spec_own[:, C:]
-    gain_in[:, :C] = weight * (ar * br + ai * bi)
-    gain_in[:, C:] = weight * (ar * bi - ai * br)
+    ar, ai, br, bi = spec_own[0:4], spec_own[4:8], grads[0:4], grads[4:8]
+    rest = jnp.zeros((4, C), F32)
+    gain_in[:, :C] = jnp.concatenate([weight * (ar * br + ai * bi), rest], axis=0)
+    gain_in[:, C:] = jnp.concatenate([weight * (ar * bi - ai * br), rest], axis=0)
     swap = remote(gain_in, gain_got, gain_s, gain_r, lat, lon, 1 - batch)
     swap.start()
 
@@ -618,14 +608,13 @@
     swap.wait()
     gain_in[...] = gain_in[...] + gain_got[...]
     for batch_at in range(2):
-        for lon_at in range(2):
-
-            @pl.when((batch == batch_at) & (lax.rem(lon, 2) == lon_at))
-            def _():
-                at = 4 * lon_at + 2 * batch_at
-                for i in range(2):
-                    for j in range(4):
-                        outg[4 * i + j : 4 * i + j + 1, :] = gain_in[at + i : at + i + 1, 128 * j : 128 * j + 128]
+
+        @pl.when(batch == batch_at)
+        def _():
+            for i in range(2):
+                for j in range(4):
+                    row = 2 * batch_at + i
+                    outg[4 * i + j : 4 * i + j + 1, :] = gain_in[row : row + 1, 128 * j : 128 * j + 128]
 
     sum1.to_owners()
     sum0.second_axis()
@@ -640,8 +629,8 @@
     for r in range(9):
         for j in range(2):
             out0[2 * r + j : 2 * r + j + 1, :] = scales[0] * t0[r : r + 1, 128 * j : 128 * j + 128]
-    first_gather.close()
-    gather.close()
+    forth.close()
+    back_way.close()
     pred_out.wait()
 
 
@@ -695,15 +684,22 @@
     cells0 = 2 * 128 * 768
     scales = (1.0 / math.sqrt(cells0), 1.0 / math.sqrt(cells0 // 4), 1.0 / math.sqrt(cells0 // 64))
     names = INPUTS
-    gathers = (dma(7), dma(8), dma(7, 4), dma(7, 4), dma(8), dma(8))
-    scratch = [vmem(32, 1024) if n == "synth" else vmem(*args[n].shape, dtype=args[n].dtype) for n in names]
+    scratch = [
+        vmem(*args[n].shape[1:]) if n in ("synth", "table") else vmem(*args[n].shape, dtype=args[n].dtype) for n in names
+    ]
+
+    def spectral_scratch(rows):
+        sems = (dma(7), dma(8), dma(15), dma(15), dma(15), dma(15))
+        modes = vmem(NLON, 8, C, dtype=F32)
+        return (vmem(NLAT, 16, C), vmem(NLON, rows, C), vmem(NLON, rows, C), modes, modes, *sems)
+
     scratch += [
         dma(len(names)), vmem(160, C), vmem(160, C), vmem(3, 48, C), vmem(3, 48, C), vmem(22, 80, C, dtype=F32), vmem(22, 64, 3 * C), vmem(18, 48, 3 * C),
         vmem(20, 64, C), vmem(10, 48, C, dtype=F32), vmem(10, 32, 3 * C), vmem(20, 48, C), vmem(20, 48, C),
         vmem(8, 32, C), vmem(8, 32, C, dtype=F32), vmem(8, 32, C, dtype=F32), vmem(16, C), vmem(16, C, dtype=F32),
         vmem(4, 2, 16, C), vmem(10, 2, 16, C), dma(8), dma(8), dma(8), dma(8),
-        vmem(8, 2, 8, 16, C), vmem(8, 2, 8, 16, C), gathers, gathers, vmem(1024, C, dtype=F32), vmem(1024, C),
-        vmem(16, C), vmem(8, 2 * C, dtype=F32), vmem(16, C), vmem(ROWS, COLS, C), dma(),
+        spectral_scratch(16), spectral_scratch(32), vmem(1024, C, dtype=F32), vmem(1024, C),
+        vmem(16, C), vmem(16, C), vmem(ROWS, COLS, C), dma(),
         vmem(10, 48, C, dtype=F32), vmem(10, 32, C, dtype=F32), vmem(10, 32, C), vmem(16, 48, C),
         vmem(C, C, dtype=F32), reduce_scratch(HALF, 48), reduce_scratch(HALF + 128, 32), vmem(8, 2 * C, dtype=F32), vmem(8, 2 * C, dtype=F32), dma(), dma(),
     ]

time: 81.8 us -> 71.1 us (0.87)
  Pallas kernels: 81.1 us -> 70.4 us
    pallas_call x1, Pallas kernels: 79.2 us -> 68.5 us  [on_device(): pl.pallas_call(functools.partial(kernel, scales, len(INPUTS)), out_shape=...]
where the time goes in v5:
time: 71.1 us; the launch traced here: 71 us
  Pallas kernels  70.4 us (99%)
    pallas_call x1, Pallas kernels, on_device(): pl.pallas_call(functools.partial(kernel, scales, len(INPUTS)), out_shape=...  68.5 us
    pallas_call x1, Pallas kernels, hand_over(): pl.pallas_call(body, out_shape=[jax.ShapeDtypeStruct(a.shape, a.dtype) fo...  1.84 us

profile of v5, /device:TPU:1, one launch (start us, length us, event | category | flops | bytes accessed | tf_op | source)
XLA Modules:
  0.0 71.0 jit_solution(2999995335031438953)
XLA Ops:
  0.6 68.5 %shard_map.218 = (bf16[16,48,256]{2,1,0:T(8,128)(2,1)}, f32[18,128]{1,0:T(8,128)}, f32[18,128]{1,0:T(8,128)}, f32[2,128]{1,0:T(2,128)}, f32[8,128]{1,0:T(8,128)}) custom-call(bf16[16,48,256]{2,1,0:T(8,128)(2,1)} %bitcast.11, bf16[160,768]{1,0:T(8,128)(2,1)} %constant.26.clone.refs_1_, bf16[16,48,256]{2,1,0:T(8,128)(2,1)} %bitcast.12, ...), custom_call_target="tpu_custom_call" | custom-call | tf_op jit(solution)/shard_map/pallas_call | solution.py:708
  69.2 1.8 %shard_map.219 = (bf16[16,48,256]{2,1,0:T(8,128)(2,1)}, f32[18,128]{1,0:T(8,128)}, f32[18,128]{1,0:T(8,128)}, f32[2,128]{1,0:T(2,128)}, f32[8,128]{1,0:T(8,128)}) custom-call(bf16[16,48,256]{2,1,0:T(8,128)(2,1)} %get-tuple-element.15.refs_0_, f32[18,128]{1,0:T(8,128)} %get-tuple-element.16.refs_1_, f32[18,128]{1,0:T(8,128)} %get-tuple-element.17.refs_2_, ...), custom_call_target="tpu_custom_call" | custom-call | tf_op jit(solution)/shard_map/pallas_call | solution.py:671

commit v6 on v5

--- a/solution.py
+++ b/solution.py
@@ -196,14 +196,14 @@
 
 def greet_all():
     lat, lon, batch = place()
-    for k in range(1, NLAT):
-        signal(step(lat, k, NLAT), lon, batch)
-    for k in range(1, NLON):
-        signal(lat, step(lon, k, NLON), batch)
     for dlat, dlon in NEIGHBOURS[4:]:
         signal(step(lat, dlat, NLAT), step(lon, dlon, NLON), batch)
+    for k in (4, 3, 5, 2, 6, 1, 7):
+        signal(step(lat, k, NLAT), lon, batch)
+    for k in Spectral.FAR_FIRST:
+        signal(lat, step(lon, k, NLON), batch)
+    signal(lat, lon + 2 - 4 * lax.rem(lon // 2, 2), 1 - batch)
     signal(lat, lon, 1 - batch)
-    signal(lat, lon + 2 - 4 * lax.rem(lon // 2, 2), 1 - batch)
     return 28
 
 
@@ -439,12 +439,30 @@
     for i, n in enumerate(names):
         ref = src[n].at[dict(synth=lat, table=lon)[n]] if n in ("synth", "table") else src[n]
         loads[n] = pltpu.make_async_copy(ref, v[n], load_sem.at[i])
-    early = ("field", "hpick", "cot", "dec", "sum8")
+    early = ("field", "hpick", "k0", "cot", "dec", "sum8")
     for n in early:
         loads[n].start()
     loads["field"].wait()
     loads["hpick"].wait()
     packed[...] = dot(v["hpick"][...], field[...].reshape(768, C)).astype(BF16)
+    fs[3:19, 16:64] = field[...].astype(F32)
+    loads["k0"].wait()
+
+    def level_rows(y, n, c0, c1):
+        size = n * (c1 - c0)
+        acc = dot(x3[pl.ds(y, n), c0:c1].reshape(size, 3 * C), k0[0])
+        acc += dot(x3[pl.ds(y + 1, n), c0:c1].reshape(size, 3 * C), k0[1])
+        acc += dot(x3[pl.ds(y + 2, n), c0:c1].reshape(size, 3 * C), k0[2])
+        act, grad = gelu_both(acc)
+        out = fs[pl.ds(y + 1, n), 8 + c0 : 8 + c1, :] + act.reshape(n, c1 - c0, C)
+        l0f[pl.ds(y, n), c0:c1] = out.astype(BF16)
+        a, b = max(c0, 8), min(c1, 56)
+        level0[pl.ds(y, n), a - 8 : b - 8] = out[:, a - c0 : b - c0].astype(BF16)
+        da0[pl.ds(y, n), a - 8 : b - 8] = grad.reshape(n, c1 - c0, C)[:, a - c0 : b - c0].astype(BF16)
+
+    for b in range(3):
+        x3[3:19, 16:48, b * C : (b + 1) * C] = fs[3:19, 23 + b : 55 + b, :].astype(BF16)
+    lax.fori_loop(0, 2, lambda i, _: (level_rows(4 + 6 * i, 6, 16, 48), 0)[1], 0)
     pl.semaphore_wait(pltpu.get_barrier_semaphore(), n_peers)
     halo = halo_copies(field, rows_top, rows_bot, packed, halo_in, halo_s, halo_r)
     for copy in halo:
@@ -461,9 +479,9 @@
         gl2[8 * half : 8 * half + 8] = dot(v["sum8"][...], part)
     c1s[...] = jnp.zeros_like(c1s)
     g1s[...] = jnp.zeros_like(g1s)
-    fs[3:19, 16:64] = field[...].astype(F32)
-    for n in ("hplace", "k0", "pool2", "k1", "pool4", "pick"):
+    for n in ("hplace", "pool2", "k1", "pool4", "pick"):
         loads[n].wait()
+
     for copy in halo:
         copy.wait()
 
@@ -477,21 +495,14 @@
         fs[3:19, at : at + 16] = sides[3:19, half : half + 16]
         fs[19:22, at : at + 16] = jnp.where(edge_bot, 0.0, sides[19:22, half : half + 16])
     for b in range(3):
-        x3[:, :, b * C : (b + 1) * C] = fs[:, 7 + b : 71 + b, :].astype(BF16)
-
-    def rows4(i, _):
-        y = 4 * i
-        acc = dot(x3[pl.ds(y, 4)].reshape(256, 3 * C), k0[0])
-        acc += dot(x3[pl.ds(y + 1, 4)].reshape(256, 3 * C), k0[1])
-        acc += dot(x3[pl.ds(y + 2, 4)].reshape(256, 3 * C), k0[2])
-        act, grad = gelu_both(acc)
-        out = fs[pl.ds(y + 1, 4), 8:72, :] + act.reshape(4, 64, C)
-        l0f[pl.ds(y, 4)] = out.astype(BF16)
-        level0[pl.ds(y, 4)] = out[:, 8:56].astype(BF16)
-        da0[pl.ds(y, 4)] = grad.reshape(4, 64, C)[:, 8:56].astype(BF16)
-        return 0
-
-    lax.fori_loop(0, 5, rows4, 0)
+        lane = slice(b * C, (b + 1) * C)
+        x3[0:3, :, lane] = fs[0:3, 7 + b : 71 + b, :].astype(BF16)
+        x3[19:22, :, lane] = fs[19:22, 7 + b : 71 + b, :].astype(BF16)
+        x3[3:19, 0:16, lane] = fs[3:19, 7 + b : 23 + b, :].astype(BF16)
+        x3[3:19, 48:64, lane] = fs[3:19, 55 + b : 71 + b, :].astype(BF16)
+    lax.fori_loop(0, 2, lambda i, _: (level_rows(16 * i, 4, 0, 64), 0)[1], 0)
+    level_rows(4, 12, 0, 16)
+    level_rows(4, 12, 48, 64)
 
     for y in range(10):
         row = dot(v["pool2"][...], l0f[2 * y : 2 * y + 2].reshape(128, C)).astype(BF16).astype(F32)
@@ -616,8 +627,8 @@
                     row = 2 * batch_at + i
                     outg[4 * i + j : 4 * i + j + 1, :] = gain_in[row : row + 1, 128 * j : 128 * j + 128]
 
+    sum0.second_axis()
     sum1.to_owners()
-    sum0.second_axis()
     sum0.to_owners()
     t1 = sum1.finish()
     for r in range(9):

time: 71.1 us -> 69 us (0.970)
  Pallas kernels: 70.4 us -> 68.2 us
    pallas_call x1, Pallas kernels: 68.5 us -> 66.4 us  [on_device(): pl.pallas_call(functools.partial(kernel, scales, len(INPUTS)), out_shape=...]
where the time goes in v6:
time: 69 us; the launch traced here: 68.8 us
  Pallas kernels  68.2 us (99%)
    pallas_call x1, Pallas kernels, on_device(): pl.pallas_call(functools.partial(kernel, scales, len(INPUTS)), out_shape=...  66.4 us
    pallas_call x1, Pallas kernels, hand_over(): pl.pallas_call(body, out_shape=[jax.ShapeDtypeStruct(a.shape, a.dtype) fo...  1.84 us

profile of v6, /device:TPU:1, one launch (start us, length us, event | category | flops | bytes accessed | tf_op | source)
XLA Modules:
  0.0 68.8 jit_solution(11187972216694190829)
XLA Ops:
  0.6 66.4 %shard_map.218 = (bf16[16,48,256]{2,1,0:T(8,128)(2,1)}, f32[18,128]{1,0:T(8,128)}, f32[18,128]{1,0:T(8,128)}, f32[2,128]{1,0:T(2,128)}, f32[8,128]{1,0:T(8,128)}) custom-call(bf16[16,48,256]{2,1,0:T(8,128)(2,1)} %bitcast.11, bf16[160,768]{1,0:T(8,128)(2,1)} %constant.26.clone.refs_1_, bf16[16,48,256]{2,1,0:T(8,128)(2,1)} %bitcast.12, ...), custom_call_target="tpu_custom_call" | custom-call | tf_op jit(solution)/shard_map/pallas_call | solution.py:719
  67.0 1.8 %shard_map.219 = (bf16[16,48,256]{2,1,0:T(8,128)(2,1)}, f32[18,128]{1,0:T(8,128)}, f32[18,128]{1,0:T(8,128)}, f32[2,128]{1,0:T(2,128)}, f32[8,128]{1,0:T(8,128)}) custom-call(bf16[16,48,256]{2,1,0:T(8,128)(2,1)} %get-tuple-element.15.refs_0_, f32[18,128]{1,0:T(8,128)} %get-tuple-element.16.refs_1_, f32[18,128]{1,0:T(8,128)} %get-tuple-element.17.refs_2_, ...), custom_call_target="tpu_custom_call" | custom-call | tf_op jit(solution)/shard_map/pallas_call | solution.py:682

commit v7 on v6

--- a/solution.py
+++ b/solution.py
@@ -562,6 +562,7 @@
     mixes[...] = mix
     sum1.out[HALF : HALF + 128, :] = mixes[pl.ds(pl.multiple_of(128 - 128 * sum1.core, 128), 128), :].astype(BF16)
     sum1.total1[HALF : HALF + 128, :] = mixes[pl.ds(pl.multiple_of(128 * sum1.core, 128), 128), :]
+    sum1.one[3][1].start()
     spec_own = forth.collect_modes()
 
     def predict(r):
@@ -588,7 +589,6 @@
     g1s[:, 8:40, :] = gp1
     gown = jnp.where((col[1:9] >= 4) & (col[1:9] < 28), gp1[1:9], 0.0).astype(BF16).reshape(256, C)
     sum1.halves(x13, gown)
-    sum1.one[3][1].start()
 
     gc1 = gl1[1:9].reshape(256, C)
     for b in range(3):
@@ -604,6 +604,8 @@
     sum1.first_axis()
     sum0.halves(x3c, gp0[...].reshape(768, C))
 
+    sum0.first_axis()
+
     grads = back_way.collect_modes()
     m = lax.rem(4 * lon + lax.broadcasted_iota(jnp.int32, (4, C), 0), 32)
     weight = jnp.where(m == 0, 1.0, 2.0)
@@ -614,8 +616,9 @@
     swap = remote(gain_in, gain_got, gain_s, gain_r, lat, lon, 1 - batch)
     swap.start()
 
-    sum0.first_axis()
     sum1.second_axis()
+    sum0.second_axis()
+    sum1.to_owners()
     swap.wait()
     gain_in[...] = gain_in[...] + gain_got[...]
     for batch_at in range(2):
@@ -627,8 +630,6 @@
                     row = 2 * batch_at + i
                     outg[4 * i + j : 4 * i + j + 1, :] = gain_in[row : row + 1, 128 * j : 128 * j + 128]
 
-    sum0.second_axis()
-    sum1.to_owners()
     sum0.to_owners()
     t1 = sum1.finish()
     for r in range(9):

time: 69 us -> 68.7 us (level)
  no operation moved by 1% of the time
where the time goes in v7:
time: 68.7 us; the launch traced here: 68.6 us
  Pallas kernels  68 us (99%)
    pallas_call x1, Pallas kernels, on_device(): pl.pallas_call(functools.partial(kernel, scales, len(INPUTS)), out_shape=...  66.1 us
    pallas_call x1, Pallas kernels, hand_over(): pl.pallas_call(body, out_shape=[jax.ShapeDtypeStruct(a.shape, a.dtype) fo...  1.84 us

profile of v7, /device:TPU:1, one launch (start us, length us, event | category | flops | bytes accessed | tf_op | source)
XLA Modules:
  0.0 68.6 jit_solution(8633591348039682207)
XLA Ops:
  0.6 66.1 %shard_map.218 = (bf16[16,48,256]{2,1,0:T(8,128)(2,1)}, f32[18,128]{1,0:T(8,128)}, f32[18,128]{1,0:T(8,128)}, f32[2,128]{1,0:T(2,128)}, f32[8,128]{1,0:T(8,128)}) custom-call(bf16[16,48,256]{2,1,0:T(8,128)(2,1)} %bitcast.11, bf16[160,768]{1,0:T(8,128)(2,1)} %constant.26.clone.refs_1_, bf16[16,48,256]{2,1,0:T(8,128)(2,1)} %bitcast.12, ...), custom_call_target="tpu_custom_call" | custom-call | tf_op jit(solution)/shard_map/pallas_call | solution.py:720
  66.8 1.8 %shard_map.219 = (bf16[16,48,256]{2,1,0:T(8,128)(2,1)}, f32[18,128]{1,0:T(8,128)}, f32[18,128]{1,0:T(8,128)}, f32[2,128]{1,0:T(2,128)}, f32[8,128]{1,0:T(8,128)}) custom-call(bf16[16,48,256]{2,1,0:T(8,128)(2,1)} %get-tuple-element.15.refs_0_, f32[18,128]{1,0:T(8,128)} %get-tuple-element.16.refs_1_, f32[18,128]{1,0:T(8,128)} %get-tuple-element.17.refs_2_, ...), custom_call_target="tpu_custom_call" | custom-call | tf_op jit(solution)/shard_map/pallas_call | solution.py:683
